TPU v7x, 32 devices: a whole 2x2x4 slice. The times are simulated.
32 devices in a mesh: ha: 4 (over y, x), wa: 2 (over core), col: 4 (over z).
Axes of the slice: x: 2, y: 2, z: 4, core: 2. Of those that a mesh axis runs over, the one named last changes fastest.
Arguments:
- features: bfloat16 [8, 32, 16, 2048], P('col', 'ha', 'wa'), may hold values from -60 to 60
- region_boxes: int32 [8, 3, 4], replicated, may hold values from 0 to 32, as said below
- branch_weight: bfloat16 [4, 2048, 512], P(None, None, 'col'), may hold values from -0.125 to 0.125
- branch_gain: float32 [4, 512], P(None, 'col'), may hold values from 0.5 to 1.5
- branch_bias: float32 [4, 512], P(None, 'col'), may hold values from -3 to 3
- conv_weight: bfloat16 [9, 4096, 512], P(None, None, 'col'), may hold values from -0.03125 to 0.03125
- norm_gain: float32 [512], P('col'), may hold values from 0.1 to 1.9
- norm_bias: float32 [512], P('col'), may hold values from -3 to 3
- class_weight: float32 [512, 19], P('col'), may hold values from -0.25 to 0.25
- class_bias: float32 [19], replicated, may hold values from -4 to 4
- cotangent: float32 [8, 32, 16, 19], P('col', 'ha', 'wa'), may hold values from -6 to 6
Outputs:
- logits: float32 [8, 32, 16, 19], P('col', 'ha', 'wa')
- feature_grad: float32 [8, 32, 16, 2048], P('col', 'ha', 'wa')
- branch_grad: float32 [4, 2048, 512], P(None, None, 'col')
- branch_gain_grad: float32 [4, 512], P(None, 'col')
- branch_bias_grad: float32 [4, 512], P(None, 'col')
- conv_grad: float32 [9, 4096, 512], P(None, ('ha', 'wa'), 'col')
- norm_gain_grad: float32 [512], P('col')
- norm_bias_grad: float32 [512], P('col')
- class_weight_grad: float32 [512, 19], P('col')
- class_bias_grad: float32 [19], replicated
Inputs may be any that keep to these rules, and one draw needn't show every extreme that they name: `region_boxes`: each canvas holds three disjoint boxes (first row, first column, end row, end column; ends excluded): box 0 = rows [0, 32), columns [0, c); box 1 = rows [0, r), columns [c, 16); box 2 = rows [r, 32), columns [c, 16 - p); with 2 <= c < 8, 2 <= r <= 30, 0 <= p < 8. Pixels outside the boxes are padding.
All inputs are finite; a program needn't handle non-finite values.
Results may differ from a plain program's by a relative error of at most 0.0095.
The roundings to bfloat16 on the way count: a program that leaves them out, or rounds other values in their place, can miss the bound.
Values may be sent and summed in bfloat16 or wider, within the bound.
A program may use at most 256 MiB of HBM per device.

v0:
```python
import jax
import jax.numpy as jnp
from jax import lax
from jax.sharding import PartitionSpec as P

EPSILON = 1e-05
LEVELS = (1, 2, 3, 6)
FULL_ACCURACY = lax.Precision.HIGHEST


def extended(block, sides, width):
    for axis, dim in sides:
        count = lax.axis_size(axis)
        forward = [(i, i + 1) for i in range(count - 1)]
        backward = [(target, source) for source, target in forward]
        low = lax.ppermute(
            lax.slice_in_dim(block, block.shape[dim] - width, None, axis=dim), axis, forward
        )
        high = lax.ppermute(lax.slice_in_dim(block, 0, width, axis=dim), axis, backward)
        block = jnp.concatenate([low, block, high], axis=dim)
    return block


def interpolate(offset, extent, n, bin_ids):
    scaled = offset * (n - 1)
    lower_bin = scaled // (extent - 1)
    fraction = (scaled - lower_bin * (extent - 1)).astype(jnp.float32) / (extent - 1).astype(
        jnp.float32
    )
    upper_bin = jnp.minimum(lower_bin + 1, n - 1)
    lower_hit = (bin_ids[None, :] == lower_bin[:, None]).astype(jnp.float32)
    upper_hit = (bin_ids[None, :] == upper_bin[:, None]).astype(jnp.float32)
    return (1.0 - fraction)[:, None] * lower_hit + fraction[:, None] * upper_hit


def layout(region, row_ids, col_ids):
    member_cols = []
    count_cols = []
    weight_per_level = []
    validity = jnp.zeros(row_ids.shape, jnp.float32)
    for n in LEVELS:
        bin_ids = jnp.arange(n, dtype=jnp.int32)
        level_weights = []
        for k in range(region.shape[0]):
            row_start = region[k, 0]
            col_start = region[k, 1]
            height = region[k, 2] - row_start
            width = region[k, 3] - col_start
            row_offset = row_ids - row_start
            col_offset = col_ids - col_start
            inside = (
                (row_offset >= 0) & (row_offset < height) & (col_offset >= 0) & (col_offset < width)
            )
            row_low = bin_ids * height // n
            row_high = ((bin_ids + 1) * height + n - 1) // n
            col_low = bin_ids * width // n
            col_high = ((bin_ids + 1) * width + n - 1) // n
            row_in = (row_offset[:, None] >= row_low[None, :]) & (
                row_offset[:, None] < row_high[None, :]
            )
            col_in = (col_offset[:, None] >= col_low[None, :]) & (
                col_offset[:, None] < col_high[None, :]
            )
            member = row_in[:, :, None] & col_in[:, None, :] & inside[:, None, None]
            member_cols.append(member.reshape(-1, n * n).astype(jnp.float32))
            count_cols.append(
                ((row_high - row_low)[:, None] * (col_high - col_low)[None, :]).reshape(n * n)
            )
            row_weight = interpolate(row_offset, height, n, bin_ids)
            col_weight = interpolate(col_offset, width, n, bin_ids)
            bilinear = (
                row_weight[:, :, None]
                * col_weight[:, None, :]
                * inside.astype(jnp.float32)[:, None, None]
            )
            level_weights.append(bilinear.reshape(-1, n * n))
            if n == 1:
                validity = validity + inside.astype(jnp.float32)
        weight_per_level.append(jnp.concatenate(level_weights, 1))
    counts = jnp.concatenate(count_cols).astype(jnp.float32)
    return (jnp.concatenate(member_cols, 1), weight_per_level, counts, validity)


def silu_slope(inputs):
    logistic = jax.nn.sigmoid(inputs)
    return logistic * (1.0 + inputs * (1.0 - logistic))


def body(
    features,
    region_boxes,
    branch_weight,
    branch_gain,
    branch_bias,
    conv_weight,
    norm_gain,
    norm_bias,
    class_weight,
    class_bias,
    cotangent,
):
    micros, tile_rows, tile_cols, channels = features.shape
    groups = lax.axis_size("col")
    regions = region_boxes.shape[1]
    share = conv_weight.shape[2]
    width_out = share * groups
    pixels = tile_rows * tile_cols
    flat_rows = groups * pixels
    col_index = lax.axis_index("col")
    tile_row_ids = lax.axis_index("ha") * tile_rows + jnp.arange(tile_rows, dtype=jnp.int32)
    tile_col_ids = lax.axis_index("wa") * tile_cols + jnp.arange(tile_cols, dtype=jnp.int32)
    row_ids = jnp.repeat(tile_row_ids, tile_cols)
    col_ids = jnp.tile(tile_col_ids, tile_rows)
    conv_flat = conv_weight.reshape(-1, share)
    conv_back = jnp.transpose(conv_weight, (0, 2, 1)).reshape(-1, conv_weight.shape[1])
    spans = [regions * n * n for n in LEVELS]
    starts = [sum(spans[:level_number]) for level_number in range(len(LEVELS))]
    grouped_boxes = region_boxes.reshape(groups, micros, regions, 4)
    branch_float = branch_weight.astype(jnp.float32)
    branch_grads = [jnp.zeros((channels, share), jnp.float32) for level_number in range(4)]
    branch_gain_grads = [jnp.zeros((share,), jnp.float32) for level_number in range(4)]
    branch_bias_grads = [jnp.zeros((share,), jnp.float32) for level_number in range(4)]
    norm_gain_total = jnp.zeros((share,), jnp.float32)
    norm_bias_total = jnp.zeros((share,), jnp.float32)
    class_weight_total = jnp.zeros(class_weight.shape, jnp.float32)
    class_bias_total = jnp.zeros(class_bias.shape, jnp.float32)
    conv_total = jnp.zeros(conv_flat.shape, jnp.float32)
    logit_list = []
    feature_list = []
    for m in range(micros):
        boxes_now = grouped_boxes[:, m]
        member_pixels, weight_per_level, counts, validity = jax.vmap(
            lambda region: layout(region, row_ids, col_ids)
        )(boxes_now)
        own_members = lax.dynamic_index_in_dim(member_pixels, col_index, 0, False)
        own_counts = lax.dynamic_index_in_dim(counts, col_index, 0, False)
        own_valid = lax.dynamic_index_in_dim(validity, col_index, 0, False)
        areas = (boxes_now[:, :, 2] - boxes_now[:, :, 0]) * (
            boxes_now[:, :, 3] - boxes_now[:, :, 1]
        )
        valid_total = jnp.sum(areas.astype(jnp.float32))
        local_x = features[m].reshape(pixels, channels)
        partial_value = jnp.einsum(
            "pb,pd->bd",
            own_members.astype(jnp.bfloat16),
            local_x,
            preferred_element_type=jnp.float32,
        )
        bin_total = lax.psum(partial_value, ("ha", "wa"))
        pooled = (bin_total / own_counts[:, None]).astype(jnp.bfloat16)
        pooled_all = lax.all_gather(pooled[None], "col", axis=0, tiled=True)
        branch_norms = []
        branch_affines = []
        branch_inverse = []
        branch_outs = []
        for level_number in range(4):
            level_pooled = pooled_all[
                :, starts[level_number] : starts[level_number] + spans[level_number]
            ]
            pre = jnp.einsum(
                "cbd,de->cbe",
                level_pooled,
                branch_weight[level_number],
                preferred_element_type=jnp.float32,
            )
            average = jnp.mean(pre, (0, 1))
            spread = jnp.mean(pre * pre, (0, 1)) - average * average
            inverse = lax.rsqrt(spread + EPSILON)
            normed_branch = (pre - average) * inverse
            affine_branch = branch_gain[level_number] * normed_branch + branch_bias[level_number]
            branch_norms.append(normed_branch)
            branch_affines.append(affine_branch)
            branch_inverse.append(inverse)
            branch_outs.append(jax.nn.silu(affine_branch))
        branch_local = jnp.concatenate(branch_outs, 1).astype(jnp.bfloat16)
        branch_full = lax.all_gather(branch_local, "col", axis=2, tiled=True)
        enlarged_map = []
        for level_number in range(4):
            level_output = branch_full[
                :, starts[level_number] : starts[level_number] + spans[level_number]
            ].astype(jnp.float32)
            spread_out = jnp.einsum(
                "zdw,zwk->zdk",
                weight_per_level[level_number],
                level_output,
                precision=FULL_ACCURACY,
            )
            enlarged_map.append(
                spread_out.reshape(groups, tile_rows, tile_cols, width_out).astype(jnp.bfloat16)
            )
        x_all = lax.all_gather(features[m][None], "col", axis=0, tiled=True)
        masked_x = x_all * validity.reshape(groups, tile_rows, tile_cols, 1).astype(jnp.bfloat16)
        stacked = jnp.concatenate([masked_x] + enlarged_map, -1)
        padded = extended(stacked, (("ha", 1), ("wa", 2)), 1)
        columns = jnp.concatenate(
            [
                padded[:, row_tap : row_tap + tile_rows, col_tap : col_tap + tile_cols]
                for row_tap in range(3)
                for col_tap in range(3)
            ],
            -1,
        ).reshape(flat_rows, -1)
        convolved = jnp.dot(columns, conv_flat, preferred_element_type=jnp.float32)
        valid_flat = validity.reshape(flat_rows, 1)
        first_sum, second_sum = lax.psum(
            (jnp.sum(convolved * valid_flat, 0), jnp.sum(convolved * convolved * valid_flat, 0)),
            ("ha", "wa"),
        )
        average = first_sum / valid_total
        spread = second_sum / valid_total - average * average
        inverse = lax.rsqrt(spread + EPSILON)
        normed = (convolved - average) * inverse
        affine = norm_gain * normed + norm_bias
        hidden = jax.nn.silu(affine)
        part_logits = jnp.dot(hidden, class_weight, precision=FULL_ACCURACY).reshape(
            groups, tile_rows, tile_cols, -1
        )
        summed = lax.psum_scatter(part_logits, "col", scatter_dimension=0, tiled=True)
        own_valid_tile = own_valid.reshape(tile_rows, tile_cols, 1)
        logit_list.append((summed[0] + class_bias) * own_valid_tile)
        seed = (cotangent[m] * own_valid_tile)[None]
        seed_all = lax.all_gather(seed, "col", axis=0, tiled=True).reshape(flat_rows, -1)
        grad_hidden = jnp.dot(seed_all, class_weight.T, precision=FULL_ACCURACY)
        grad_affine = grad_hidden * silu_slope(affine)
        bias_sum, gain_sum, class_part, bias_part = lax.psum(
            (
                jnp.sum(grad_affine, 0),
                jnp.sum(grad_affine * normed, 0),
                jnp.dot(hidden.T, seed_all, precision=FULL_ACCURACY),
                jnp.sum(seed_all, 0),
            ),
            ("ha", "wa"),
        )
        norm_bias_total = norm_bias_total + bias_sum
        norm_gain_total = norm_gain_total + gain_sum
        class_weight_total = class_weight_total + class_part
        class_bias_total = class_bias_total + bias_part
        grad_conv = (
            valid_flat
            * inverse
            * (
                grad_affine * norm_gain
                - norm_gain * bias_sum / valid_total
                - normed * norm_gain * gain_sum / valid_total
            )
        )
        grad_low = grad_conv.astype(jnp.bfloat16)
        grad_pad = extended(
            grad_low.reshape(groups, tile_rows, tile_cols, share), (("ha", 1), ("wa", 2)), 1
        )
        grad_columns = jnp.concatenate(
            [
                grad_pad[
                    :, 2 - row_tap : 2 - row_tap + tile_rows, 2 - col_tap : 2 - col_tap + tile_cols
                ]
                for row_tap in range(3)
                for col_tap in range(3)
            ],
            -1,
        ).reshape(flat_rows, -1)
        grad_stacked = jnp.dot(grad_columns, conv_back, preferred_element_type=jnp.float32)
        conv_part = jnp.einsum("pk,pe->ke", columns, grad_low, preferred_element_type=jnp.float32)
        conv_total = conv_total + conv_part
        grad_x = grad_stacked[:, :channels]
        bin_parts = []
        for level_number in range(4):
            level_gradient = grad_stacked[
                :, channels + level_number * width_out : channels + (level_number + 1) * width_out
            ].reshape(groups, pixels, width_out)
            bin_parts.append(
                jnp.einsum(
                    "qkl,qko->qlo",
                    weight_per_level[level_number],
                    level_gradient,
                    precision=FULL_ACCURACY,
                )
            )
        bin_local = jnp.concatenate(bin_parts, 1)
        bin_grad = lax.psum(bin_local, ("ha", "wa", "col"))
        own_bin_grad = lax.dynamic_slice_in_dim(bin_grad, col_index * share, share, 2)
        grad_pres = []
        for level_number in range(4):
            grad_out = own_bin_grad[
                :, starts[level_number] : starts[level_number] + spans[level_number]
            ]
            grad_act = grad_out * silu_slope(branch_affines[level_number])
            act_sum = jnp.sum(grad_act, (0, 1))
            act_norm_sum = jnp.sum(grad_act * branch_norms[level_number], (0, 1))
            samples = float(groups * spans[level_number])
            branch_bias_grads[level_number] = branch_bias_grads[level_number] + act_sum
            branch_gain_grads[level_number] = branch_gain_grads[level_number] + act_norm_sum
            grad_pre = branch_inverse[level_number] * (
                branch_gain[level_number] * grad_act
                - branch_gain[level_number] * act_sum / samples
                - branch_norms[level_number] * branch_gain[level_number] * act_norm_sum / samples
            )
            level_pooled = pooled_all[
                :, starts[level_number] : starts[level_number] + spans[level_number]
            ].astype(jnp.float32)
            branch_grads[level_number] = branch_grads[level_number] + jnp.einsum(
                "cbd,cbe->de", level_pooled, grad_pre, precision=FULL_ACCURACY
            )
            grad_pres.append(grad_pre)
        pooled_grads = [
            jnp.einsum(
                "cbe,de->cbd",
                grad_pres[level_number],
                branch_float[level_number],
                precision=FULL_ACCURACY,
            )
            for level_number in range(4)
        ]
        grad_pooled = jnp.concatenate(pooled_grads, 1)
        back_x, back_pooled = (
            lax.psum_scatter(
                grad_x.reshape(groups, pixels, channels).astype(jnp.bfloat16),
                "col",
                scatter_dimension=0,
                tiled=True,
            ).astype(jnp.float32),
            lax.psum_scatter(
                grad_pooled.astype(jnp.bfloat16), "col", scatter_dimension=0, tiled=True
            ).astype(jnp.float32),
        )
        pooled_back = back_pooled[0]
        spread_back = jnp.dot(
            own_members, pooled_back / own_counts[:, None], precision=FULL_ACCURACY
        )
        feature_list.append(
            (back_x[0] * own_valid[:, None] + spread_back).reshape(tile_rows, tile_cols, channels)
        )
    conv_result = lax.psum_scatter(
        conv_total.reshape(9, -1, share), ("ha", "wa"), scatter_dimension=1, tiled=True
    )
    return (
        jnp.stack(logit_list),
        jnp.stack(feature_list),
        jnp.stack(branch_grads),
        jnp.stack(branch_gain_grads),
        jnp.stack(branch_bias_grads),
        conv_result,
        norm_gain_total,
        norm_bias_total,
        class_weight_total,
        class_bias_total,
    )


def solution(mesh):
    placed = (
        P("col", "ha", "wa", None),
        P(),
        P(None, None, "col"),
        P(None, "col"),
        P(None, "col"),
        P(None, None, "col"),
        P("col"),
        P("col"),
        P("col", None),
        P(),
        P("col", "ha", "wa", None),
    )
    return jax.shard_map(
        body,
        mesh=mesh,
        in_specs=placed,
        out_specs=(
            P("col", "ha", "wa", None),
            P("col", "ha", "wa", None),
            P(None, None, "col"),
            P(None, "col"),
            P(None, "col"),
            P(None, ("ha", "wa"), "col"),
            P("col"),
            P("col"),
            P("col", None),
            P(),
        ),
        check_vma=False,
    )
```

profile of v0, /device:TPU:8, one launch (start us, length us, event | category | flops | bytes accessed | tf_op | source)
XLA Modules:
  0.0 918.7 jit_solution(2643051222730832738)
XLA Ops:
  44.9 51.5 %all-reduce.9.cloned.1.call-done = (f32[150,2048]{1,0:T(8,128)}, f32[150,2048]{1,0:T(8,128)}) async-done(((f32[150,2048]{1,0:T(8,128)}, f32[150,2048]{1,0:T(8,128)}), (f32[150,2048]{1,0:T(8,128)}, f32[150,2048]{1,0:T(8,128)})) %all-reduce.9.cloned.1.call-update) | async-done | bytes 2457616 | tf_op jit(solution)/shard_map/psum | solution.py:149
  96.4 2.4 fusion.37
  109.1 2.4 multiply_dynamic-update-slice_fusion.3
  113.0 36.3 %all-gather.15.cloned.1.call-done = bf16[4,150,2048]{2,1,0:T(8,128)(2,1)} async-done(((bf16[1,150,2048]{2,1,0:T(8,128)(2,1)}), bf16[4,150,2048]{2,1,0:T(8,128)(2,1)}) %all-gather.15.cloned.1.call-update) | async-done | bytes 2457616 | tf_op jit(solution)/shard_map/all_gather | solution.py:151
  149.3 1.9 fusion.728
  151.8 51.1 %all-gather.13.cloned.1.call-done = bf16[4,150,2048]{2,1,0:T(8,128)(2,1)} async-done(((bf16[1,150,2048]{2,1,0:T(8,128)(2,1)}), bf16[4,150,2048]{2,1,0:T(8,128)(2,1)}) %all-gather.13.cloned.1.call-update) | async-done | bytes 2457616 | tf_op jit(solution)/shard_map/all_gather | solution.py:151
  211.8 16.9 %all_gather.26 = bf16[4,150,512]{2,1,0:T(8,128)(2,1)S(1)} all-gather(bf16[4,150,128]{2,1,0:T(8,128)(2,1)S(1)} %pad_maximum_fusion.20), channel_id=1, replica_groups=mesh['ha'=4,'wa'=2,'col'=4] {'col'}, dimensions={2}, use_global_device_ids=true | all-gather | bytes 768000 | tf_op jit(solution)/shard_map/all_gather | solution.py:176
  230.6 3.4 collective-permute-start
  235.4 14.7 %all_gather.29 = bf16[4,150,512]{2,1,0:T(8,128)(2,1)S(1)} all-gather(bf16[4,150,128]{2,1,0:T(8,128)(2,1)S(1)} %pad_maximum_fusion.21), channel_id=1, replica_groups=mesh['ha'=4,'wa'=2,'col'=4] {'col'}, dimensions={2}, use_global_device_ids=true | all-gather | bytes 768000 | tf_op jit(solution)/shard_map/all_gather | solution.py:176
  254.7 4.6 collective-permute-start.4
  265.5 3.2 collective-permute-done.5
  275.8 11.4 %pad_maximum_fusion = (bf16[4,10,9,4096]{3,2,1,0:T(8,128)(2,1)S(1)}, bf16[4,10,9,4096]{3,2,1,0:T(8,128)(2,1)S(1)}) fusion(bf16[4,10,1,4096]{3,2,1,0:T(2,128)(2,1)S(1)} %copy.459, bf16[4,1,8,4096]{3,2,1,0:T(8,128)(2,1)S(1)} %collective-permute-done.1, bf16[4,8,8,4096]{3,2,1,0:T(8,128)(2,1)S(1)} %get-tuple-element.859, ...), kind=kLoop, calls=%fused_computation.2 | loop fusion | flops 23592960 | bytes 9175040 | tf_op jit(solution)/shard_map/concatenate | solution.py:20
  292.0 2.1 copy.510
  294.1 6.7 pad_maximum_fusion.1
  300.8 2.0 slice_dynamic-update-slice_fusion.5
  308.8 18.5 %multiply_reduce_fusion.8 = (f32[128]{0:T(128)S(1)}, f32[128]{0:T(128)S(1)}, f32[256,128]{1,0:T(8,128)S(1)}) fusion(f32[256]{0:T(256)S(1)} %copy-done.90, bf16[256,36864]{1,0:T(8,128)(2,1)} %bitcast.347, bf16[36864,128]{1,0:T(8,128)(2,1)} %bitcast.345), kind=kOutput, calls=%fused_computation.259 | convolution fusion | flops 2416082944 | bytes 28444672 | tf_op jit(solution)/shard_map/dot_general | solution.py:203
  327.3 8.4 multiply_reduce_fusion.6
  335.7 15.4 %all-reduce.2 = (f32[128]{0:T(128)S(1)}, f32[128]{0:T(128)S(1)}, f32[128]{0:T(128)S(1)}, f32[128]{0:T(128)S(1)}) all-reduce(f32[128]{0:T(128)S(1)} %get-tuple-element.22, f32[128]{0:T(128)S(1)} %get-tuple-element.21, f32[128]{0:T(128)S(1)} %get-tuple-element.20, ...), channel_id=1, replica_groups=mesh['ha'=4,'wa'=2,'col'=4] {'ha','wa'}, use_global_device_ids=true, to_apply=%region_25.27 | all-reduce | flops 512 | bytes 4096 | tf_op jit(solution)/shard_map/psum | solution.py:205
  355.7 12.2 %copy.512 = bf16[9,4096,128]{1,2,0:T(8,128)(2,1)} copy(bf16[9,4096,128]{2,1,0:T(8,128)(2,1)} %param.18) | data formatting | bytes 18874368 | tf_op args[5]
  368.1 20.1 %reduce-scatter.10.cloned.1.call-done = f32[1,8,8,19]{3,2,1,0:T(8,128)} async-done(((f32[4,8,8,19]{3,2,1,0:T(8,128)}), f32[1,8,8,19]{3,2,1,0:T(8,128)}) %reduce-scatter.10.cloned.1.call-update) | async-done | bytes 4880 | tf_op jit(solution)/shard_map/reduce_scatter | solution.py:218
  389.7 13.5 %all_gather.30 = f32[4,8,8,19]{3,2,1,0:T(8,128)S(1)} all-gather(f32[1,8,8,19]{3,2,1,0:T(8,128)S(1)} %get-tuple-element.291), channel_id=1, replica_groups=mesh['ha'=4,'wa'=2,'col'=4] {'col'}, dimensions={0}, use_global_device_ids=true | all-gather | bytes 24320 | tf_op jit(solution)/shard_map/all_gather | solution.py:222
  403.8 13.4 %all_gather.31 = f32[4,8,8,19]{3,2,1,0:T(8,128)S(1)} all-gather(f32[1,8,8,19]{3,2,1,0:T(8,128)S(1)} %get-tuple-element.292), channel_id=1, replica_groups=mesh['ha'=4,'wa'=2,'col'=4] {'col'}, dimensions={0}, use_global_device_ids=true | all-gather | bytes 24320 | tf_op jit(solution)/shard_map/all_gather | solution.py:222
  417.9 22.9 %all-reduce.1 = (f32[128]{0:T(128)S(1)}, f32[128]{0:T(128)S(1)}, f32[128]{0:T(128)S(1)}, f32[128]{0:T(128)S(1)}, f32[128,19]{0,1:T(8,128)}, /*index=5*/f32[19]{0:T(128)}) all-reduce(f32[128]{0:T(128)S(1)} %get-tuple-element.26, f32[128]{0:T(128)S(1)} %get-tuple-element.25, ...), channel_id=1, replica_groups=mesh['ha'=4,'wa'=2,'col'=4] {'ha','wa'}, use_global_device_ids=true, to_apply=%region_48.50 | all-reduce | flops 2963 | bytes 23704 | tf_op jit(solution)/shard_map/psum | solution.py:225
  440.8 1.8 fusion.783
  446.7 6.3 collective-permute-start.12
  455.7 3.0 collective-permute-start.11
  460.8 3.0 collective-permute-start.15
  464.3 6.2 fusion.784
  474.4 2.9 fusion.785
  483.1 2.9 slice.1109
  486.2 148.4 %all-reduce.7.cloned.1.call-done = (f32[4,150,512]{2,1,0:T(8,128)}, f32[4,150,512]{2,1,0:T(8,128)}) async-done(((f32[4,150,512]{2,1,0:T(8,128)}, f32[4,150,512]{2,1,0:T(8,128)}), (f32[4,150,512]{2,1,0:T(8,128)}, f32[4,150,512]{2,1,0:T(8,128)})) %all-reduce.7.cloned.1.call-update) | async-done | bytes 2457616 | tf_op jit(solution)/shard_map/psum | solution.py:279
  636.2 2.2 fusion.717
  639.3 1.9 fusion.711
  646.3 2.3 convolution_convert_fusion.1
  648.6 2.3 pad_maximum_fusion.3
  651.0 2.7 slice.1108
  657.2 2.3 convolution_convert_fusion
  659.5 2.4 pad_maximum_fusion.4
  661.9 12.8 %fusion.786 = f32[36864,128]{1,0:T(8,128)} fusion(bf16[256,36864]{1,0:T(8,128)(2,1)} %bitcast.348, bf16[256,128]{1,0:T(8,128)(2,1)S(1)} %get-tuple-element.612), kind=kOutput, calls=%fused_computation.1930 | convolution fusion | flops 2415919104 | bytes 37814272 | tf_op jit(solution)/shard_map/pk,pe->ke/dot_general | solution.py:262
  674.8 21.8 %convolution_add_fusion = f32[36864,128]{1,0:T(8,128)} fusion(f32[36864,128]{1,0:T(8,128)} %fusion.786, bf16[256,36864]{1,0:T(8,128)(2,1)} %bitcast.344, bf16[256,128]{1,0:T(8,128)(2,1)S(1)} %get-tuple-element.613), kind=kOutput, calls=%fused_computation | convolution fusion | flops 2420637696 | bytes 56688640 | tf_op jit(solution)/shard_map/pk,pe->ke/dot_general | solution.py:262
  707.3 2.6 convolution_bitcast_fusion
  710.0 2.6 fusion.7
  712.6 2.3 pad_maximum_fusion.2
  714.9 1.9 fusion.8
  716.9 10.7 %reduce-scatter.16.cloned.1.call-done = bf16[1,64,2048]{2,1,0:T(8,128)(2,1)} async-done(((bf16[4,64,2048]{2,1,0:T(8,128)(2,1)}), bf16[1,64,2048]{2,1,0:T(8,128)(2,1)}) %reduce-scatter.16.cloned.1.call-update) | async-done | bytes 262160 | tf_op jit(solution)/shard_map/reduce_scatter | solution.py:315
  727.5 52.1 %reduce-scatter.18.cloned.1.call-done = bf16[1,150,2048]{2,1,0:T(8,128)(2,1)} async-done(((bf16[4,150,2048]{2,1,0:T(8,128)(2,1)}), bf16[1,150,2048]{2,1,0:T(8,128)(2,1)}) %reduce-scatter.18.cloned.1.call-update) | async-done | bytes 614416 | tf_op jit(solution)/shard_map/reduce_scatter | solution.py:321
  779.6 1.9 fusion.9
  782.6 128.1 %reduce-scatter.20.cloned.1.call-done = f32[9,512,128]{2,1,0:T(8,128)} async-done(((f32[9,4096,128]{2,1,0:T(8,128)}), f32[9,512,128]{2,1,0:T(8,128)}) %reduce-scatter.20.cloned.1.call-update) | async-done | bytes 2359312 | tf_op jit(solution)/shard_map/reduce_scatter | solution.py:332
  (911 shorter events, 135.7 us)
Async XLA Ops:
  8.0 343.8 %copy-start = (f32[128,19]{0,1:T(8,128)S(1)}, f32[128,19]{0,1:T(8,128)}, u32[]{:S(2)}) copy-start(f32[128,19]{0,1:T(8,128)} %param.21) | copy-start | bytes 29188
  8.0 88.4 %all-reduce.9.cloned.1.call-start = ((), (), s32[]{:S(2)}) async-start(), calls=%async_computation.19 | async-start | bytes 4980736 | tf_op jit(solution)/shard_map/psum | solution.py:149
  31.3 77.7 %all-gather.9.cloned.1.call-start = ((), (), s32[]{:S(2)}) async-start(), calls=%async_computation.7 | async-start | bytes 1310720 | tf_op jit(solution)/shard_map/all_gather | solution.py:191
  32.2 79.3 %all-gather.11.cloned.1.call-start = ((), (), s32[]{:S(2)}) async-start(), calls=%async_computation.9 | async-start | bytes 1310720 | tf_op jit(solution)/shard_map/all_gather | solution.py:191
  32.8 116.5 %all-gather.15.cloned.1.call-start = ((), (), s32[]{:S(2)}) async-start(), calls=%async_computation.17 | async-start | bytes 3112960 | tf_op jit(solution)/shard_map/all_gather | solution.py:151
  98.9 104.0 %all-gather.13.cloned.1.call-start = ((), (), s32[]{:S(2)}) async-start(), calls=%async_computation.16 | async-start | bytes 3112960 | tf_op jit(solution)/shard_map/all_gather | solution.py:151
  102.6 265.5 %reduce-scatter.8.cloned.1.call-start = ((), (), s32[]{:S(2)}) async-start(), calls=%async_computation.8 | async-start | bytes 163840 | tf_op jit(solution)/shard_map/reduce_scatter | solution.py:218
  230.6 29.9 %collective-permute-start = (bf16[4,1,8,4096]{3,2,1,0:T(8,128)(2,1)S(1)}, bf16[4,1,8,4096]{3,2,1,0:T(8,128)(2,1)S(1)}, u32[]{:S(2)}, u32[]{:S(2)}) collective-permute-start(bf16[4,1,8,4096]{3,2,1,0:T(8,128)(2,1)S(1)} %get-tuple-element.257), channel_id=1, source_target_pairs={{0,8},{8,16},{16,24},{1,9},{9,17},{17,25},{2,10},{10,18},{18,26},{... | collective-permute-start | bytes 786440 | tf_op jit(solution)/shard_map/ppermute | solution.py:16
  234.1 26.5 %collective-permute-start.1 = (bf16[4,1,8,4096]{3,2,1,0:T(8,128)(2,1)S(1)}, bf16[4,1,8,4096]{3,2,1,0:T(8,128)(2,1)S(1)}, u32[]{:S(2)}, u32[]{:S(2)}) collective-permute-start(bf16[4,1,8,4096]{3,2,1,0:T(8,128)(2,1)S(1)} %get-tuple-element.258), channel_id=1, source_target_pairs={{8,0},{16,8},{24,16},{9,1},{17,9},{25,17},{10,2},{18,10},{26,18},{... | collective-permute-start | bytes 786440 | tf_op jit(solution)/shard_map/ppermute | solution.py:19
  254.7 10.8 %collective-permute-start.4 = (bf16[4,1,8,4096]{3,2,1,0:T(8,128)(2,1)S(1)}, bf16[4,1,8,4096]{3,2,1,0:T(8,128)(2,1)S(1)}, u32[]{:S(2)}, u32[]{:S(2)}) collective-permute-start(bf16[4,1,8,4096]{3,2,1,0:T(8,128)(2,1)S(1)} %get-tuple-element.259), channel_id=1, source_target_pairs={{0,8},{8,16},{16,24},{1,9},{9,17},{17,25},{2,10},{10,18},{18,26},{... | collective-permute-start | bytes 786440 | tf_op jit(solution)/shard_map/ppermute | solution.py:16
  259.3 9.5 %collective-permute-start.5 = (bf16[4,1,8,4096]{3,2,1,0:T(8,128)(2,1)S(1)}, bf16[4,1,8,4096]{3,2,1,0:T(8,128)(2,1)S(1)}, u32[]{:S(2)}, u32[]{:S(2)}) collective-permute-start(bf16[4,1,8,4096]{3,2,1,0:T(8,128)(2,1)S(1)} %get-tuple-element.260), channel_id=1, source_target_pairs={{8,0},{16,8},{24,16},{9,1},{17,9},{25,17},{10,2},{18,10},{26,18},{... | collective-permute-start | bytes 786440 | tf_op jit(solution)/shard_map/ppermute | solution.py:19
  262.5 11.9 %collective-permute-start.2 = (bf16[4,10,1,4096]{3,1,2,0:T(8,128)(2,1)S(1)}, bf16[4,10,1,4096]{3,1,2,0:T(8,128)(2,1)S(1)}, u32[]{:S(2)}, u32[]{:S(2)}) collective-permute-start(bf16[4,10,1,4096]{3,1,2,0:T(8,128)(2,1)S(1)} %copy.456), channel_id=1, source_target_pairs={{0,4},{1,5},{2,6},{3,7},{8,12},{9,13},{10,14},{11,15},{16,20},{17,... | collective-permute-start | bytes 983048 | tf_op jit(solution)/shard_map/ppermute | solution.py:16
  264.2 10.9 %collective-permute-start.3 = (bf16[4,10,1,4096]{3,1,2,0:T(8,128)(2,1)S(1)}, bf16[4,10,1,4096]{3,1,2,0:T(8,128)(2,1)S(1)}, u32[]{:S(2)}, u32[]{:S(2)}) collective-permute-start(bf16[4,10,1,4096]{3,1,2,0:T(8,128)(2,1)S(1)} %copy.458), channel_id=1, source_target_pairs={{4,0},{5,1},{6,2},{7,3},{12,8},{13,9},{14,10},{15,11},{20,16},{21,... | collective-permute-start | bytes 983048 | tf_op jit(solution)/shard_map/ppermute | solution.py:19
  270.6 20.7 %collective-permute-start.6 = (bf16[4,10,1,4096]{3,1,2,0:T(8,128)(2,1)S(1)}, bf16[4,10,1,4096]{3,1,2,0:T(8,128)(2,1)S(1)}, u32[]{:S(2)}, u32[]{:S(2)}) collective-permute-start(bf16[4,10,1,4096]{3,1,2,0:T(8,128)(2,1)S(1)} %copy.507), channel_id=1, source_target_pairs={{0,4},{1,5},{2,6},{3,7},{8,12},{9,13},{10,14},{11,15},{16,20},{17,... | collective-permute-start | bytes 983048 | tf_op jit(solution)/shard_map/ppermute | solution.py:16
  273.1 18.9 %collective-permute-start.7 = (bf16[4,10,1,4096]{3,1,2,0:T(8,128)(2,1)}, bf16[4,10,1,4096]{3,1,2,0:T(8,128)(2,1)}, u32[]{:S(2)}, u32[]{:S(2)}) collective-permute-start(bf16[4,10,1,4096]{3,1,2,0:T(8,128)(2,1)} %copy.509), channel_id=1, source_target_pairs={{4,0},{5,1},{6,2},{7,3},{12,8},{13,9},{14,10},{15,11},{20,16},{21,... | collective-permute-start | bytes 983048 | tf_op jit(solution)/shard_map/ppermute | solution.py:19
  352.8 35.4 %reduce-scatter.10.cloned.1.call-start = ((), (), s32[]{:S(2)}) async-start(), calls=%async_computation.10 | async-start | bytes 163840 | tf_op jit(solution)/shard_map/reduce_scatter | solution.py:218
  354.5 280.1 %all-reduce.7.cloned.1.call-start = ((), (), s32[]{:S(2)}) async-start(), calls=%async_computation.18 | async-start | bytes 4980736 | tf_op jit(solution)/shard_map/psum | solution.py:279
  444.1 10.2 %collective-permute-start.8 = (bf16[4,1,8,128]{3,2,1,0:T(8,128)(2,1)S(1)}, bf16[4,1,8,128]{3,2,1,0:T(8,128)(2,1)S(1)}, u32[]{:S(2)}, u32[]{:S(2)}) collective-permute-start(bf16[4,1,8,128]{3,2,1,0:T(8,128)(2,1)S(1)} %get-tuple-element.285), channel_id=1, source_target_pairs={{0,8},{8,16},{16,24},{1,9},{9,17},{17,25},{2,10},{10,18},{18,26},{... | collective-permute-start | bytes 24584 | tf_op jit(solution)/shard_map/ppermute | solution.py:16
  445.4 8.9 collective-permute-start.9
  446.7 12.0 %collective-permute-start.12 = (bf16[4,1,8,128]{3,2,1,0:T(8,128)(2,1)S(1)}, bf16[4,1,8,128]{3,2,1,0:T(8,128)(2,1)S(1)}, u32[]{:S(2)}, u32[]{:S(2)}) collective-permute-start(bf16[4,1,8,128]{3,2,1,0:T(8,128)(2,1)S(1)} %get-tuple-element.289), channel_id=1, source_target_pairs={{0,8},{8,16},{16,24},{1,9},{9,17},{17,25},{2,10},{10,18},{18,26},{... | collective-permute-start | bytes 24584 | tf_op jit(solution)/shard_map/ppermute | solution.py:16
  453.0 6.4 collective-permute-start.13
  454.4 9.5 %collective-permute-start.10 = (bf16[4,10,1,128]{3,2,1,0:T(2,128)(2,1)S(1)}, bf16[4,10,1,128]{3,2,1,0:T(2,128)(2,1)S(1)}, u32[]{:S(2)}, u32[]{:S(2)}) collective-permute-start(bf16[4,10,1,128]{3,2,1,0:T(2,128)(2,1)S(1)} %get-tuple-element.278), channel_id=1, source_target_pairs={{4,0},{5,1},{6,2},{7,3},{12,8},{13,9},{14,10},{15,11},{20,16},{21,... | collective-permute-start | bytes 30728 | tf_op jit(solution)/shard_map/ppermute | solution.py:19
  455.7 8.2 collective-permute-start.11
  459.5 14.4 %collective-permute-start.14 = (bf16[4,10,1,128]{3,2,1,0:T(2,128)(2,1)S(1)}, bf16[4,10,1,128]{3,2,1,0:T(2,128)(2,1)S(1)}, u32[]{:S(2)}, u32[]{:S(2)}) collective-permute-start(bf16[4,10,1,128]{3,2,1,0:T(2,128)(2,1)S(1)} %get-tuple-element.282), channel_id=1, source_target_pairs={{4,0},{5,1},{6,2},{7,3},{12,8},{13,9},{14,10},{15,11},{20,16},{21,... | collective-permute-start | bytes 30728 | tf_op jit(solution)/shard_map/ppermute | solution.py:19
  460.8 13.1 %collective-permute-start.15 = (bf16[4,10,1,128]{3,2,1,0:T(2,128)(2,1)S(1)}, bf16[4,10,1,128]{3,2,1,0:T(2,128)(2,1)S(1)}, u32[]{:S(2)}, u32[]{:S(2)}) collective-permute-start(bf16[4,10,1,128]{3,2,1,0:T(2,128)(2,1)S(1)} %get-tuple-element.281), channel_id=1, source_target_pairs={{0,4},{1,5},{2,6},{3,7},{8,12},{9,13},{10,14},{11,15},{16,20},{17,... | collective-permute-start | bytes 30728 | tf_op jit(solution)/shard_map/ppermute | solution.py:16
  481.6 154.6 %copy-start.20 = (f32[4,27,128]{2,1,0:T(8,128)S(1)}, f32[4,27,128]{2,1,0:T(8,128)}, u32[]{:S(2)}) copy-start(f32[4,27,128]{2,1,0:T(8,128)} %copy-done.19) | copy-start | bytes 165892
  481.6 154.6 %copy-start.78 = (f32[128]{0:T(128)S(1)}, f32[128]{0:T(128)}, u32[]{:S(2)}) copy-start(f32[128]{0:T(128)} %get-tuple-element.905) | copy-start | bytes 1540
  481.6 154.6 %copy-start.95 = (f32[128]{0:T(128)S(1)}, f32[128]{0:T(128)}, u32[]{:S(2)}) copy-start(f32[128]{0:T(128)} %copy-done.94) | copy-start | bytes 1540
  481.6 154.5 %copy-start.98 = (f32[128]{0:T(128)S(1)}, f32[128]{0:T(128)}, u32[]{:S(2)}) copy-start(f32[128]{0:T(128)} %copy-done.97) | copy-start | bytes 1540
  482.9 155.6 %copy-start.41 = (f32[4,3,128]{2,1,0:T(4,128)S(1)}, f32[4,3,128]{2,1,0:T(4,128)}, u32[]{:S(2)}) copy-start(f32[4,3,128]{2,1,0:T(4,128)} %get-tuple-element.843) | copy-start | bytes 18436
  482.9 155.6 %copy-start.43 = (f32[4,3,128]{2,1,0:T(4,128)S(1)}, f32[4,3,128]{2,1,0:T(4,128)}, u32[]{:S(2)}) copy-start(f32[4,3,128]{2,1,0:T(4,128)} %copy-done.42) | copy-start | bytes 18436
  482.9 155.6 %copy-start.93 = (f32[128]{0:T(128)S(1)}, f32[128]{0:T(128)}, u32[]{:S(2)}) copy-start(f32[128]{0:T(128)} %get-tuple-element.908) | copy-start | bytes 1540
  482.9 155.6 %copy-start.113 = (f32[128]{0:T(128)S(1)}, f32[128]{0:T(128)}, u32[]{:S(2)}) copy-start(f32[128]{0:T(128)} %get-tuple-element.828) | copy-start | bytes 1540
  482.9 155.6 %copy-start.115 = (f32[128]{0:T(128)S(1)}, f32[128]{0:T(128)}, u32[]{:S(2)}) copy-start(f32[128]{0:T(128)} %get-tuple-element.829) | copy-start | bytes 1540
  482.9 155.6 %copy-start.117 = (f32[128]{0:T(128)S(1)}, f32[128]{0:T(128)}, u32[]{:S(2)}) copy-start(f32[128]{0:T(128)} %copy-done.116) | copy-start | bytes 1540
  482.9 155.6 %copy-start.119 = (f32[128]{0:T(128)S(1)}, f32[128]{0:T(128)}, u32[]{:S(2)}) copy-start(f32[128]{0:T(128)} %copy-done.118) | copy-start | bytes 1540
  482.9 155.6 %copy-start.137 = (f32[128]{0:T(128)S(1)}, f32[128]{0:T(128)}, u32[]{:S(2)}) copy-start(f32[128]{0:T(128)} %get-tuple-element.451) | copy-start | bytes 1540
  482.9 156.4 %copy-start.86 = (f32[128]{0:T(128)S(1)}, f32[128]{0:T(128)}, u32[]{:S(2)}) copy-start(f32[128]{0:T(128)} %get-tuple-element.906) | copy-start | bytes 1540
  482.9 156.4 %copy-start.123 = (f32[128]{0:T(128)S(1)}, f32[128]{0:T(128)}, u32[]{:S(2)}) copy-start(f32[128]{0:T(128)} %copy-done.122) | copy-start | bytes 1540
  483.0 156.4 %copy-start.126 = (f32[128]{0:T(128)S(1)}, f32[128]{0:T(128)}, u32[]{:S(2)}) copy-start(f32[128]{0:T(128)} %copy-done.125) | copy-start | bytes 1540
  483.0 158.3 %copy-start.121 = (f32[4,128]{1,0:T(4,128)S(1)}, f32[4,128]{1,0:T(4,128)}, u32[]{:S(2)}) copy-start(f32[4,128]{1,0:T(4,128)} %param.16) | copy-start | bytes 6148
  483.0 160.1 %copy-start.8 = (bf16[4,2048,128]{2,1,0:T(8,128)(2,1)S(1)}, bf16[4,2048,128]{2,1,0:T(8,128)(2,1)}, u32[]{:S(2)}) copy-start(bf16[4,2048,128]{2,1,0:T(8,128)(2,1)} %param.15) | copy-start | bytes 6291460
  483.0 231.9 %reduce-scatter.12.cloned.1.call-start = ((), (), s32[]{:S(2)}) async-start(), calls=%async_computation.11 | async-start | bytes 1310720 | tf_op jit(solution)/shard_map/reduce_scatter | solution.py:315
  486.0 229.0 %reduce-scatter.14.cloned.1.call-start = ((), (), s32[]{:S(2)}) async-start(), calls=%async_computation.12 | async-start | bytes 3112960 | tf_op jit(solution)/shard_map/reduce_scatter | solution.py:321
  650.9 76.6 %reduce-scatter.16.cloned.1.call-start = ((), (), s32[]{:S(2)}) async-start(), calls=%async_computation.13 | async-start | bytes 1310720 | tf_op jit(solution)/shard_map/reduce_scatter | solution.py:315
  653.7 125.9 %reduce-scatter.18.cloned.1.call-start = ((), (), s32[]{:S(2)}) async-start(), calls=%async_computation.14 | async-start | bytes 3112960 | tf_op jit(solution)/shard_map/reduce_scatter | solution.py:321
  661.9 248.8 %reduce-scatter.20.cloned.1.call-start = ((), (), s32[]{:S(2)}) async-start(), calls=%async_computation.15 | async-start | bytes 21233664 | tf_op jit(solution)/shard_map/reduce_scatter | solution.py:332
  714.9 195.8 %copy-start.1 = (f32[128,19]{0,1:T(8,128)S(1)}, f32[128,19]{0,1:T(8,128)}, u32[]{:S(2)}) copy-start(f32[128,19]{0,1:T(8,128)} %param.21) | copy-start | bytes 29188
  (166 other events, 3311.4 us)
Sparse Core Ops, SparseCore 0:
  31.4 64.9 all-reduce.8
  483.1 151.4 all-reduce.6
Sparse Core Ops, SparseCore 1:
  33.3 29.0 all-gather.8
  63.8 27.2 all-gather.10
  98.9 50.3 all-gather.14
  151.5 51.2 all-gather.12
  352.9 14.9 reduce-scatter.7
  370.7 17.4 reduce-scatter.9
  486.0 31.4 reduce-scatter.11
  651.0 48.0 reduce-scatter.13
  701.8 25.7 reduce-scatter.15
  730.0 49.6 reduce-scatter.17
  784.1 126.5 reduce-scatter.19
where the time goes:
time: 929 us; the launch traced here: 919 us
  waiting for transfers between devices  503 us (54%)
  matrix products  124 us (13%)
  blocking collectives  96.8 us (10%)
  other arithmetic  83 us (9%)
  local copies, waits for them, and re-layouts  55.6 us (6%)
  starting transfers between devices  35.5 us (4%)
  between operations  20.7 us (2%)
    psum x1, waiting for transfers between devices, body(): bin_grad = lax.psum(bin_local, ('ha', 'wa', 'col'))  148 us
    reduce_scatter x1, waiting for transfers between devices, body(): lax.psum_scatter(conv_total.reshape(9, -1, share), ('ha', 'wa'), scatter_...  128 us
    all_gather x2, waiting for transfers between devices, body(): pooled_all = lax.all_gather(pooled[None], 'col', axis=0, tiled=True)  87.4 us
    reduce_scatter x2, waiting for transfers between devices, body(): lax.psum_scatter(grad_pooled.astype(jnp.bfloat16), 'col', scatter_dimensi...  52.1 us
    psum x1, waiting for transfers between devices, body(): bin_total = lax.psum(partial_value, ('ha', 'wa'))  51.5 us
    dot_general x2, matrix products, body(): jnp.einsum('pk,pe->ke', columns, grad_low, preferred_element_type=jnp.flo...  34.6 us
    all_gather x2, blocking collectives, body(): branch_full = lax.all_gather(branch_local, 'col', axis=2, tiled=True)  31.6 us
    all_gather x2, blocking collectives, body(): lax.all_gather(seed, 'col', axis=0, tiled=True).reshape(flat_rows, -1)  26.9 us
  transfers between devices with their start and end apart: 29, of which 10 were waited for; matrix products, arithmetic and copies ran while one was open for 18% of the time, Pallas kernels for 0%

commit v1 on v0

--- a/solution.py
+++ b/solution.py
@@ -1,11 +1,969 @@
+import functools
+
 import jax
 import jax.numpy as jnp
+import numpy as np
 from jax import lax
+from jax.experimental import pallas as pl
+from jax.experimental.pallas import tpu as pltpu
 from jax.sharding import PartitionSpec as P
 
 EPSILON = 1e-05
 LEVELS = (1, 2, 3, 6)
 FULL_ACCURACY = lax.Precision.HIGHEST
+MESH = pl.DeviceIdType.MESH
+
+
+SPANS = (16, 16, 32, 112)
+STARTS = (0, 16, 32, 64)
+BINS = 176
+WIDE = 112
+TAPS = 9
+
+
+def whole_canvas_plan(mesh):
+    return mesh.shape["ha"] == 4 and mesh.shape["wa"] == 2 and mesh.shape["col"] == 4
+
+
+def bin_tables():
+    lanes = np.zeros((4, 8, 128), np.float32)
+    rows = np.zeros((5, BINS, 128), np.float32)
+    rows[3] = 1.0
+    for level, n in enumerate(LEVELS):
+        lanes[level, 3, :] = n - 1
+        for k in range(3):
+            for i in range(n):
+                for j in range(n):
+                    b = (k * n + i) * n + j
+                    lanes[level, :3, b] = (k, i, j)
+                    lanes[level, 4, b] = 1.0
+                    row = STARTS[level] + b
+                    for at, value in enumerate((k, i, j, n, 1.0)):
+                        rows[at, row] = value
+    return lanes, rows
+
+
+def dot(a, b, dims=((1,), (0,)), precision=None):
+    return lax.dot_general(a, b, (dims, ((), ())), precision=precision, preferred_element_type=jnp.float32)
+
+
+ROWS_T = ((0,), (0,))
+BOTH_LAST = ((1,), (1,))
+
+
+def halves(value):
+    high = value.astype(jnp.bfloat16)
+    return high, (value - high.astype(jnp.float32)).astype(jnp.bfloat16)
+
+
+def pick3(index, values):
+    return jnp.where(index == 0.0, values[0], jnp.where(index == 1.0, values[1], values[2]))
+
+
+class Sems:
+    def __init__(self):
+        self.count = 0
+
+    def take(self, n=1):
+        at = self.count
+        self.count += n
+        return at
+
+
+def head_kernel(
+    boxes, lane_table, row_table, feat, seeds, wconv, wbranch, bgain, bbias, ngain, nbias, cwt,
+    logits_out, fgrad_out, bgrad_out, small_out, cgrad_out,
+    x, lv, wall, wb, uh, ul, mt, cnt, po, pre, prr, bos, bo, val, yp, p, cr, gc, g9, gp3,
+    dxf, sbu, sbd, rxu, rxd, gb, grr, gpre, gpa, gps, gpr, dw, dwr, bg, bgr, bgh, seed_in, sd, lt, ltr, lts,
+    st, str_, small, smr, nb_s, af_s, cn_s, bga, fg, sems,
+):
+    f32, bf16 = jnp.float32, jnp.bfloat16
+    q, w, z = lax.axis_index("ha"), lax.axis_index("wa"), lax.axis_index("col")
+    xq, yq = lax.rem(q, 2), lax.div(q, 2)
+    g = 2 * xq + yq
+    zm = lax.div(z, 2)
+    zz = z * (1 - zm) + (3 - z) * zm
+    names = Sems()
+    later = []
+
+    def peer(kx, ky, kw):
+        px = xq + kx - 2 * kx * xq
+        py = yq + ky - 2 * ky * yq
+        return {"ha": 2 * py + px, "wa": w + kw - 2 * kw * w}, 2 * px + py
+
+    def copy(src, dst, ss, rs, dev):
+        return pltpu.make_async_remote_copy(
+            src_ref=src, dst_ref=dst, send_sem=sems.at[ss], recv_sem=sems.at[rs], device_id=dev, device_id_type=MESH
+        )
+
+    def zpeer(j):
+        return {"col": lax.rem(z + j, 4)}
+
+    plane = [(kx, ky, kw) for kw in (0, 1) for ky in (0, 1) for kx in (0, 1) if kx + ky + kw]
+    chips = [(1, 0), (0, 1), (1, 1)]
+
+    g512 = pl.multiple_of(g * 512, 512)
+    weight_copies = []
+    for t in range(TAPS):
+        for part in range(2):
+            s = names.take()
+            weight_copies.append(
+                pltpu.make_async_copy(
+                    wconv.at[t, pl.ds(2048 * part + g512, 512), :],
+                    wall.at[pl.ds(512 * part, 512), pl.ds(128 * t, 128)],
+                    sems.at[s],
+                )
+            )
+    s = names.take()
+    weight_copies.append(pltpu.make_async_copy(wbranch.at[:, pl.ds(g512, 512), :], wb, sems.at[s]))
+    for c in weight_copies:
+        c.start()
+
+    prr[...] = jnp.zeros(prr.shape, f32)
+    grr[...] = jnp.zeros(grr.shape, bf16)
+    bo[...] = jnp.zeros(bo.shape, bf16)
+    yp[:, 0:8, :] = jnp.zeros((2, 8, 1152), f32)
+    yp[:, 264:272, :] = jnp.zeros((2, 8, 1152), f32)
+    gp3[:, :, 0:8, :] = jnp.zeros((3, 2, 8, 128), f32)
+    gp3[:, :, 264:272, :] = jnp.zeros((3, 2, 8, 128), f32)
+    small[...] = jnp.zeros(small.shape, f32)
+    st[...] = jnp.zeros(st.shape, f32)
+
+    barrier = pltpu.get_barrier_semaphore()
+    for kx, ky, kw in plane:
+        pl.semaphore_signal(barrier, 1, device_id=peer(kx, ky, kw)[0], device_id_type=MESH)
+    for j in (1, 2, 3):
+        pl.semaphore_signal(barrier, 1, device_id=zpeer(j), device_id_type=MESH)
+    pl.semaphore_wait(barrier, 10)
+
+    q64 = pl.multiple_of(64 * q, 64)
+    a_send, a_recv = names.take(8), names.take(8)
+    a_copies = []
+    own_row = pl.multiple_of(256 * w + 64 * q, 64)
+    for n, (kx, ky, kw) in enumerate(plane):
+        dev, block = peer(kx, ky, kw)
+        c = copy(
+            feat.at[dev["wa"], :, pl.ds(pl.multiple_of(512 * block, 512), 512)],
+            x.at[z, pl.ds(own_row, 64), :],
+            a_send + n, a_recv + n, dev,
+        )
+        c.start()
+        a_copies.append(c)
+    own = pltpu.make_async_copy(feat.at[w, :, pl.ds(g512, 512)], x.at[z, pl.ds(own_row, 64), :], sems.at[a_send + 7])
+    own.start()
+    sc_send, sc_recv = names.take(), names.take()
+    seed_copy = copy(seeds.at[1 - w], seed_in.at[0], sc_send, sc_recv, peer(0, 0, 1)[0])
+    seed_copy.start()
+
+    def scalars(canvas):
+        index = 2 * canvas + w
+        return [[boxes[index * 12 + 4 * k + e] for k in range(3)] for e in range(4)]
+
+    def px(rows, lanes, axis, start=0):
+        at = lax.broadcasted_iota(jnp.int32, (rows, lanes), axis) + start
+        half = at // 256
+        return (at // 8 % 32).astype(f32), (half * 8 + at % 8).astype(f32)
+
+    def layout(c):
+        top, left, bottom, right = [[v.astype(f32) for v in values] for values in scalars(c)]
+        y, xx = px(512, 128, 0)
+        ok = jnp.zeros((512, 128), f32)
+        for k in range(3):
+            ok = jnp.where((y >= top[k]) & (y < bottom[k]) & (xx >= left[k]) & (xx < right[k]), 1.0, ok)
+        val[c] = ok
+        table = lane_table[g]
+        box, bi, bj, n1, real = [table[e:e + 1] for e in range(5)]
+        t_, l_, b_, r_ = [pick3(box, v) for v in (top, left, bottom, right)]
+        h1, w1 = b_ - t_ - 1.0, r_ - l_ - 1.0
+        rw = jnp.maximum(1.0 - jnp.abs((y - t_) * n1 - bi * h1) / h1, 0.0)
+        cw = jnp.maximum(1.0 - jnp.abs((xx - l_) * n1 - bj * w1) / w1, 0.0)
+        inside = (y >= t_) & (y < b_) & (xx >= l_) & (xx < r_) & (real > 0.0)
+        weights = jnp.where(inside, rw * cw, 0.0)
+        high, low = halves(weights)
+        uh[c] = high
+        ul[c] = low
+        box, bi, bj, n, real = [row_table[e] for e in range(5)]
+        t_, l_, b_, r_ = [pick3(box, v) for v in (top, left, bottom, right)]
+        h, wd = b_ - t_, r_ - l_
+        row_low = jnp.floor((bi * h + 0.5) / n)
+        row_high = jnp.floor(((bi + 1.0) * h + n - 0.5) / n)
+        col_low = jnp.floor((bj * wd + 0.5) / n)
+        col_high = jnp.floor(((bj + 1.0) * wd + n - 0.5) / n)
+        cnt[c] = jnp.where(real > 0.0, (row_high - row_low) * (col_high - col_low), 1.0)
+        for chunk in range(4):
+            y, xx = px(BINS, 128, 1, 128 * chunk)
+            u, v = y - t_, xx - l_
+            member = (u >= row_low) & (u < row_high) & (v >= col_low) & (v < col_high) & (real > 0.0)
+            mt[c, :, 128 * chunk:128 * chunk + 128] = jnp.where(member, 1.0, 0.0).astype(bf16)
+
+    def combine():
+        out = []
+        zs = []
+        for b in range(3):
+            acc = [None, None]
+            for h in range(2):
+                for a in range(3):
+                    t = 3 * a + b
+                    piece = yp[h, 8 * a:8 * a + 256, 128 * t:128 * t + 128]
+                    acc[h] = piece if acc[h] is None else acc[h] + piece
+            zs.append(acc)
+        col = lax.broadcasted_iota(jnp.int32, (256, 128), 0) % 8
+        first, last = col == 0, col == 7
+        out0 = zs[1][0] + jnp.where(first, 0.0, pltpu.roll(zs[0][0], 1, 0))
+        out0 = out0 + jnp.where(last, pltpu.roll(zs[2][1], 7, 0), pltpu.roll(zs[2][0], 255, 0))
+        out1 = zs[1][1] + jnp.where(first, pltpu.roll(zs[0][0], 249, 0), pltpu.roll(zs[0][1], 1, 0))
+        out1 = out1 + jnp.where(last, 0.0, pltpu.roll(zs[2][1], 255, 0))
+        return out0, out1
+
+    def conv_part(operand, part):
+        for h in range(2):
+            yp[h, 8:264, :] = dot(operand[256 * h:256 * h + 256], wall[512 * part:512 * part + 512, :])
+        return combine()
+
+    e_send, e_recv = names.take(16), names.take(12)
+
+    def pre_copy(level, c, kx, ky):
+        slot = kx + 2 * ky - 1
+        return copy(
+            pre.at[c, pl.ds(STARTS[level], SPANS[level]), :],
+            prr.at[slot, c, pl.ds(0, SPANS[level]), :],
+            e_send + 4 * level + c, e_recv + 4 * slot + c, peer(kx, ky, 0)[0],
+        )
+
+    def to_level_owner(level, action):
+        lx, ly = level // 2, level % 2
+        for kx, ky in chips:
+            wanted = (xq + kx - 2 * kx * xq == lx) & (yq + ky - 2 * ky * yq == ly)
+            pl.when(wanted)(functools.partial(action, kx, ky))
+
+    def process(c):
+        po_sum = dot(mt[c], x[c])
+        for chunk in range(4):
+            po[c, :, 128 * chunk:128 * chunk + 128] = (po_sum[:, 128 * chunk:128 * chunk + 128] / cnt[c]).astype(bf16)
+        for level in range(4):
+            rows = slice(STARTS[level], STARTS[level] + SPANS[level])
+            pre[c, rows, :] = dot(po[c, rows, :], wb[level])
+        for level in range(4):
+            to_level_owner(level, lambda kx, ky, level=level: pre_copy(level, c, kx, ky).start())
+        out0, out1 = conv_part(x[c], 0)
+        p[c, 0] = out0
+        p[c, 1] = out1
+
+    for c in range(4):
+        layout(c)
+
+    for c in weight_copies:
+        c.wait()
+    for c in a_copies:
+        c.wait_recv()
+    own.wait()
+    ok = val[z]
+    for chunk in range(4):
+        cols = slice(128 * chunk, 128 * chunk + 128)
+        x[z, :, cols] = (x[z, :, cols].astype(f32) * ok).astype(bf16)
+
+    up_send, up_recv, dn_send, dn_recv = names.take(3), names.take(3), names.take(3), names.take(3)
+
+    def up_copy(k):
+        return copy(x.at[z - k], x.at[z - k], up_send + k, up_recv + k, {"col": z + 1})
+
+    def dn_copy(k):
+        return copy(x.at[z + k], x.at[z + k], dn_send + k, dn_recv + k, {"col": z - 1})
+
+    def up_wait(k):
+        copy(x.at[z - k], x.at[z - k], up_send + k - 1, up_recv + k - 1, {"col": z}).wait_recv()
+
+    def dn_wait(k):
+        copy(x.at[z + k], x.at[z + k], dn_send + k - 1, dn_recv + k - 1, {"col": z}).wait_recv()
+
+    pl.when(z < 3)(lambda: up_copy(0).start())
+    pl.when(z > 0)(lambda: dn_copy(0).start())
+
+    seed_copy.wait_recv()
+    sd[z] = seeds[w] + seed_in[0]
+    sz_send, sz_recv = names.take(3), names.take(3)
+    for j in (1, 2, 3):
+        copy(sd.at[z], sd.at[z], sz_send + j - 1, sz_recv + j - 1, zpeer(j)).start()
+
+    process(z)
+    for k in (1, 2, 3):
+
+        @pl.when(z >= k)
+        def _():
+            up_wait(k)
+            if k < 3:
+                pl.when(z < 3)(lambda: up_copy(k).start())
+
+        @pl.when(z + k <= 3)
+        def _():
+            dn_wait(k)
+            if k < 3:
+                pl.when(z > 0)(lambda: dn_copy(k).start())
+
+        pl.when(z >= k)(lambda: process(z - k))
+        pl.when(z + k <= 3)(lambda: process(z + k))
+
+    for c in range(4):
+        for kx, ky in chips:
+            slot = kx + 2 * ky - 1
+            for level in range(4):
+
+                @pl.when(g == level)
+                def _():
+                    copy(
+                        pre.at[c, pl.ds(STARTS[level], SPANS[level]), :],
+                        prr.at[slot, c, pl.ds(0, SPANS[level]), :],
+                        e_send, e_recv + 4 * slot + c, peer(0, 0, 1)[0],
+                    ).wait_recv()
+
+    nb_s[...] = jnp.zeros(nb_s.shape, f32)
+    for level in range(4):
+
+        @pl.when(g == level)
+        def _():
+            for c in range(4):
+                nb_s[c, 0:SPANS[level], :] = pre[c, STARTS[level]:STARTS[level] + SPANS[level], :]
+
+    level_n = jnp.where(g == 0, 1.0, jnp.where(g == 1, 2.0, jnp.where(g == 2, 3.0, 6.0)))
+    samples = 12.0 * level_n * level_n
+
+    def rows_of(value):
+        return value.reshape(4 * WIDE, 128)
+
+    pre_all = rows_of(nb_s[...] + prr[0] + prr[1] + prr[2])
+    average = jnp.sum(pre_all, 0, keepdims=True) / samples
+    spread = jnp.sum(pre_all * pre_all, 0, keepdims=True) / samples - average * average
+    b_inverse = lax.rsqrt(spread + EPSILON)
+    b_gain = bgain[pl.ds(g, 1), :]
+    b_norm = (pre_all - average) * b_inverse
+    b_act = b_gain * b_norm + bbias[pl.ds(g, 1), :]
+    nb_s[...] = b_norm.reshape(4, WIDE, 128)
+    logistic = jax.nn.sigmoid(b_act)
+    af_s[...] = (logistic * (1.0 + b_act * (1.0 - logistic))).reshape(4, WIDE, 128)
+    bos[...] = (b_act * logistic).astype(bf16).reshape(4, WIDE, 128)
+
+    f_send, f_recv = names.take(3), names.take(3)
+
+    def share(ref, at):
+        return ref.at[:, pl.ds(0, WIDE), pl.ds(pl.multiple_of(128 * at, 128), 128)]
+
+    for j in (1, 2, 3):
+        copy(bos, share(bo, z), f_send + j - 1, f_recv + j - 1, zpeer(j)).start()
+    bo[:, 0:WIDE, pl.ds(pl.multiple_of(128 * z, 128), 128)] = bos[...]
+    for j in (1, 2, 3):
+        copy(bos, share(bo, lax.rem(z + 4 - j, 4)), f_send + j - 1, f_recv + j - 1, zpeer(j)).wait_recv()
+
+    i_send, i_recv = names.take(12), names.take(12)
+
+    def chip_rows(at):
+        return pl.ds(pl.multiple_of(64 * at, 64), 64)
+
+    def conv_copy(c, kx, ky):
+        slot = kx + 2 * ky - 1
+        dev, _ = peer(kx, ky, 0)
+        return copy(p.at[c, :, chip_rows(dev["ha"]), :], cr.at[slot, c], i_send + 4 * slot + c, i_recv + 4 * slot + c, dev)
+
+    def level_conv(c, carry):
+        lv[c] = (dot(uh[c], bo[c]) + dot(ul[c], bo[c])).astype(bf16)
+        out0, out1 = conv_part(lv[c], 1)
+        p[c, 0] = p[c, 0] + out0
+        p[c, 1] = p[c, 1] + out1
+        for kx, ky in chips:
+            conv_copy(c, kx, ky).start()
+        return carry
+
+    lax.fori_loop(0, 4, level_conv, 0)
+
+    for j in (1, 2, 3):
+        src = lax.rem(z + 4 - j, 4)
+        copy(sd.at[src], sd.at[src], sz_send + j - 1, sz_recv + j - 1, zpeer(j)).wait_recv()
+    for c in range(4):
+        cn_s[0, 128 * c:128 * c + 128, :] = dot(sd[c], cwt[...], ROWS_T, FULL_ACCURACY)
+
+    for c in range(4):
+        for kx, ky in chips:
+            conv_copy(c, kx, ky).wait_recv()
+    convolved = (p[:, :, pl.ds(q64, 64), :] + cr[0] + cr[1] + cr[2]).reshape(512, 128)
+    ok = val.at[...].reshape(4, 2, 256, 128)[:, :, pl.ds(q64, 64), :].reshape(512, 128)
+
+    j_send, j_recv = names.take(6), names.take(6)
+
+    def stat_copy(stage, kx, ky):
+        slot = kx + 2 * ky - 1
+        return copy(
+            st.at[stage], str_.at[stage, slot], j_send + 3 * stage + slot, j_recv + 3 * stage + slot, peer(kx, ky, 0)[0]
+        )
+
+    def plane_sum(stage, first, second):
+        st[stage, 0:1, :] = first
+        st[stage, 1:2, :] = second
+        for kx, ky in chips:
+            stat_copy(stage, kx, ky).start()
+        for kx, ky in chips:
+            stat_copy(stage, kx, ky).wait_recv()
+        total = st[stage] + str_[stage, 0] + str_[stage, 1] + str_[stage, 2]
+        return total[0:1], total[1:2]
+
+    masked = convolved * ok
+    first, second = plane_sum(0, jnp.sum(masked, 0, keepdims=True), jnp.sum(convolved * masked, 0, keepdims=True))
+    area = jnp.int32(0)
+    for c in range(4):
+        top, left, bottom, right = scalars(c)
+        for k in range(3):
+            area = area + (bottom[k] - top[k]) * (right[k] - left[k])
+    valid_total = area.astype(f32)
+    average = first / valid_total
+    spread = second / valid_total - average * average
+    inverse = lax.rsqrt(spread + EPSILON)
+    normed = (convolved - average) * inverse
+    gain = ngain[...]
+    affine = gain * normed + nbias[...]
+    logistic = jax.nn.sigmoid(affine)
+    hidden = affine * logistic
+    grad_affine = cn_s[0] * (logistic * (1.0 + affine * (1.0 - logistic)))
+    part_bias = jnp.sum(grad_affine, 0, keepdims=True)
+    part_gain = jnp.sum(grad_affine * normed, 0, keepdims=True)
+    cn_s[1] = hidden
+    small[48:49, :] = part_bias
+    small[49:50, :] = part_gain
+    bias_sum, gain_sum = plane_sum(1, part_bias, part_gain)
+    grad_conv = ok * inverse * (
+        grad_affine * gain - gain * bias_sum / valid_total - normed * gain * gain_sum / valid_total
+    )
+    gc[:, :, pl.ds(q64, 64), :] = grad_conv.astype(bf16).reshape(4, 2, 64, 128)
+    k_send, k_recv = names.take(3), names.take(3)
+
+    def gc_copy(kx, ky, at):
+        slot = kx + 2 * ky - 1
+        block = gc.at[:, :, chip_rows(at), :]
+        return copy(block, block, k_send + slot, k_recv + slot, peer(kx, ky, 0)[0])
+
+    for kx, ky in chips:
+        gc_copy(kx, ky, q).start()
+
+    lt_send, lt_recv = names.take(3), names.take(3)
+    weight_part = jnp.zeros((24, 128), f32)
+    bias_part = jnp.zeros((24, 1), f32)
+    for c in range(4):
+        hidden_c = cn_s[1, 128 * c:128 * c + 128, :]
+        lt[c] = dot(cwt[...], hidden_c, BOTH_LAST, FULL_ACCURACY)
+        weight_part = weight_part + dot(sd[c], hidden_c, precision=FULL_ACCURACY)
+        bias_part = bias_part + jnp.sum(sd[c], 1, keepdims=True)
+    small[0:24, :] = weight_part
+    small[24:48, :] = jnp.broadcast_to(bias_part, (24, 128))
+    for j in (1, 2, 3):
+        copy(lt.at[lax.rem(z + j, 4)], ltr.at[j - 1], lt_send + j - 1, lt_recv + j - 1, zpeer(j)).start()
+
+    for kx, ky in chips:
+        gc_copy(kx, ky, peer(kx, ky, 0)[0]["ha"]).wait_recv()
+
+    def shifted(c):
+        col = lax.broadcasted_iota(jnp.int32, (256, 128), 0) % 8
+        first, last = col == 0, col == 7
+        g0, g1 = gc[c, 0].astype(f32), gc[c, 1].astype(f32)
+        gp3[1, 0, 8:264, :] = g0
+        gp3[1, 1, 8:264, :] = g1
+        gp3[0, 0, 8:264, :] = jnp.where(last, pltpu.roll(g1, 7, 0), pltpu.roll(g0, 255, 0))
+        gp3[0, 1, 8:264, :] = jnp.where(last, 0.0, pltpu.roll(g1, 255, 0))
+        gp3[2, 0, 8:264, :] = jnp.where(first, 0.0, pltpu.roll(g0, 1, 0))
+        gp3[2, 1, 8:264, :] = jnp.where(first, pltpu.roll(g0, 249, 0), pltpu.roll(g1, 1, 0))
+        for a in range(3):
+            for b in range(3):
+                t = 3 * a + b
+                for h in range(2):
+                    start = 8 * (2 - a)
+                    g9[c, 256 * h:256 * h + 256, 128 * t:128 * t + 128] = gp3[b, h, start:start + 256, :].astype(bf16)
+
+    def data_grad(c):
+        shifted(c)
+        for h in range(2):
+            dxf[c, 256 * h:256 * h + 256, :] = dot(g9[c, 256 * h:256 * h + 256, :], wall[0:512, :], BOTH_LAST)
+        back = dot(g9[c], wall[512:1024, :], BOTH_LAST)
+        high, low = halves(back)
+        total = dot(uh[c], high, ROWS_T) + dot(uh[c], low, ROWS_T) + dot(ul[c], high, ROWS_T)
+        gb[c] = total[0:WIDE].astype(bf16)
+
+    ru_send, ru_recv, rd_send, rd_recv = names.take(3), names.take(3), names.take(3), names.take(3)
+
+    def ru_copy(k):
+        return copy(sbu.at[k], rxu.at[k], ru_send + k, ru_recv + k, {"col": z + 1})
+
+    def rd_copy(k):
+        return copy(sbd.at[k], rxd.at[k], rd_send + k, rd_recv + k, {"col": z - 1})
+
+    def up_on(k):
+        return (z + 3 - k <= 3) & (z < 3)
+
+    def dn_on(k):
+        return (z - 3 + k >= 0) & (z > 0)
+
+    def scatter_step(k):
+        @pl.when(up_on(k))
+        def _():
+            value = dxf[z + 3 - k]
+            if k:
+                sbu[k] = value.astype(bf16)
+
+                @pl.when(z > 0)
+                def _():
+                    ru_copy(k - 1).wait_recv()
+                    sbu[k] = (value + rxu[k - 1].astype(f32)).astype(bf16)
+            else:
+                sbu[k] = value.astype(bf16)
+            ru_copy(k).start()
+
+        @pl.when(dn_on(k))
+        def _():
+            value = dxf[z - 3 + k]
+            if k:
+                sbd[k] = value.astype(bf16)
+
+                @pl.when(z < 3)
+                def _():
+                    rd_copy(k - 1).wait_recv()
+                    sbd[k] = (value + rxd[k - 1].astype(f32)).astype(bf16)
+            else:
+                sbd[k] = value.astype(bf16)
+            rd_copy(k).start()
+
+    def canvas_at(i):
+        low = (3 - i) if i < 2 else zz * (i - 2) + (1 - zz) * (3 - i)
+        return (1 - zm) * low + zm * (3 - low)
+
+    for i in range(4):
+        data_grad(canvas_at(i))
+        if i == 0:
+            scatter_step(0)
+
+    n_send, n_recv = names.take(3), names.take(3)
+    for level in range(4):
+
+        @pl.when(g == level)
+        def _():
+            for j in (1, 2, 3):
+                at = lax.rem(z + j, 4)
+                copy(
+                    gb.at[:, pl.ds(0, SPANS[level]), pl.ds(pl.multiple_of(128 * at, 128), 128)],
+                    grr.at[j - 1, :, pl.ds(0, SPANS[level]), :],
+                    n_send + j - 1, n_recv + j - 1, zpeer(j),
+                ).start()
+
+    scatter_step(1)
+
+    def weight_grad(part, store):
+        for tile in range(2):
+            cols = slice(256 * tile, 256 * tile + 256)
+
+            def of(operand):
+                total = None
+                for c in range(4):
+                    piece = dot(operand[c, :, cols], g9[c], ROWS_T)
+                    total = piece if total is None else total + piece
+                store(tile, total)
+
+            pl.when(part == 0)(lambda: of(x))
+            pl.when(part == 1)(lambda: of(lv))
+
+    def store_out(tile, total):
+        dw[0, 256 * tile:256 * tile + 256, :] = total
+
+    def store_own(tile, total):
+        dw[1, 256 * tile:256 * tile + 256, :] = total
+
+    weight_grad(1 - w, store_out)
+    w_send, w_recv = names.take(), names.take()
+    dw_copy = copy(dw.at[0], dwr, w_send, w_recv, peer(0, 0, 1)[0])
+    dw_copy.start()
+    weight_grad(w, store_own)
+
+    for level in range(4):
+
+        @pl.when(g == level)
+        def _():
+            for j in (1, 2, 3):
+                copy(
+                    gb.at[:, pl.ds(0, SPANS[level]), pl.ds(0, 128)],
+                    grr.at[j - 1, :, pl.ds(0, SPANS[level]), :],
+                    n_send + j - 1, n_recv + j - 1, zpeer(j),
+                ).wait_recv()
+
+    own_grad = gb[:, :, pl.ds(pl.multiple_of(128 * z, 128), 128)].astype(f32)
+    for j in range(3):
+        own_grad = own_grad + grr[j].astype(f32)
+    grad_act = rows_of(own_grad) * rows_of(af_s[...])
+    b_norm = rows_of(nb_s[...])
+    act_sum = jnp.sum(grad_act, 0, keepdims=True)
+    act_norm_sum = jnp.sum(grad_act * b_norm, 0, keepdims=True)
+    small[50:51, :] = act_norm_sum
+    small[51:52, :] = act_sum
+    grad_pre = b_inverse * (
+        b_gain * grad_act - b_gain * act_sum / samples - b_norm * b_gain * act_norm_sum / samples
+    )
+    gpre[...] = grad_pre.reshape(4, WIDE, 128)
+    o_send, o_recv = names.take(3), names.take(12)
+    for level in range(4):
+
+        @pl.when(g == level)
+        def _():
+            rows = pl.ds(STARTS[level], SPANS[level])
+            for kx, ky in chips:
+                slot = kx + 2 * ky - 1
+                copy(
+                    gpre.at[:, pl.ds(0, SPANS[level]), :], gpa.at[:, rows, :],
+                    o_send + slot, o_recv + 3 * level + slot, peer(kx, ky, 0)[0],
+                ).start()
+            gpa[:, STARTS[level]:STARTS[level] + SPANS[level], :] = gpre[:, 0:SPANS[level], :]
+
+    s_send, s_recv = names.take(7), names.take(7)
+
+    def small_copy(n):
+        return copy(small, smr.at[n], s_send + n, s_recv + n, peer(*plane[n])[0])
+
+    for n in range(7):
+        small_copy(n).start()
+
+    dw_copy.wait_recv()
+    dw[1] = dw[1] + dwr[...]
+    y_send, y_recv = names.take(9), names.take(9)
+    y_dev = peer(0, 1, 1)[0]
+
+    def tap_copy(t):
+        return copy(dw.at[1, :, pl.ds(128 * t, 128)], cgrad_out.at[t], y_send + t, y_recv + t, y_dev)
+
+    def tap_own(t):
+        return pltpu.make_async_copy(dw.at[1, :, pl.ds(128 * t, 128)], cgrad_out.at[t], sems.at[y_send + t])
+
+    @pl.when(w == yq)
+    def _():
+        for t in range(TAPS):
+            tap_own(t).start()
+
+    @pl.when(w != yq)
+    def _():
+        for t in range(TAPS):
+            tap_copy(t).start()
+
+    for level in range(4):
+        lx, ly = level // 2, level % 2
+        for kx, ky in chips:
+
+            @pl.when((xq + kx - 2 * kx * xq == lx) & (yq + ky - 2 * ky * yq == ly))
+            def _():
+                slot = kx + 2 * ky - 1
+                copy(
+                    gpre.at[:, pl.ds(0, SPANS[level]), :],
+                    gpa.at[:, pl.ds(STARTS[level], SPANS[level]), :],
+                    o_send + slot, o_recv + 3 * level + slot, peer(kx, ky, 0)[0],
+                ).wait_recv()
+
+    def pooled_grad(c, carry):
+        for level in range(4):
+            rows = slice(STARTS[level], STARTS[level] + SPANS[level])
+            high, low = halves(gpa[c, rows, :])
+            gps[c, rows, :] = (dot(high, wb[level], BOTH_LAST) + dot(low, wb[level], BOTH_LAST)).astype(bf16)
+        return carry
+
+    lax.fori_loop(0, 4, pooled_grad, 0)
+    p_send, p_recv = names.take(3), names.take(3)
+    for j in (1, 2, 3):
+        copy(gps.at[lax.rem(z + j, 4)], gpr.at[j - 1], p_send + j - 1, p_recv + j - 1, zpeer(j)).start()
+
+    scatter_step(2)
+
+    for level in range(4):
+        rows = slice(STARTS[level], STARTS[level] + SPANS[level])
+        total = None
+        for c in range(4):
+            high, low = halves(gpa[c, rows, :])
+            piece = dot(po[c, rows, :], high, ROWS_T) + dot(po[c, rows, :], low, ROWS_T)
+            total = piece if total is None else total + piece
+        bg[level] = total
+    bc_send, bc_recv = names.take(), names.take()
+    w256 = pl.multiple_of(256 * w, 256)
+    v256 = pl.multiple_of(256 * (1 - w), 256)
+    bg_copy = copy(bg.at[:, pl.ds(v256, 256), :], bgr, bc_send, bc_recv, peer(0, 0, 1)[0])
+    bg_copy.start()
+    bg_copy.wait_recv()
+    bgh[...] = (bg[:, pl.ds(w256, 256), :] + bgr[...]).astype(bf16)
+    own_channels = pl.ds(pl.multiple_of(512 * g + 256 * w, 256), 256)
+    bx_send, bx_recv = names.take(3), names.take(3)
+    by_send, by_recv = names.take(4), names.take(4)
+
+    def bga_of(block, core):
+        return bga.at[:, pl.ds(pl.multiple_of(512 * block + 256 * core, 256), 256), :]
+
+    def bg_chip(kx, ky):
+        slot = kx + 2 * ky - 1
+        return copy(bgh, bga_of(g, w), bx_send + slot, bx_recv + slot, peer(kx, ky, 0)[0])
+
+    def bg_core(n, block):
+        return copy(bga_of(block, w), bga_of(block, w), by_send + n, by_recv + n, peer(0, 0, 1)[0])
+
+    for kx, ky in chips:
+        bg_chip(kx, ky).start()
+    bga[:, own_channels, :] = bgh[...]
+    bg_core(3, g).start()
+
+    for j in (1, 2, 3):
+        copy(lt.at[0], ltr.at[j - 1], lt_send + j - 1, lt_recv + j - 1, zpeer(j)).wait_recv()
+    lts[w] = lt[z] + ltr[0] + ltr[1] + ltr[2]
+    ls_send, ls_recv = names.take(), names.take()
+    logits_copy = copy(lts.at[w], lts.at[w], ls_send, ls_recv, peer(0, 0, 1)[0])
+    logits_copy.start()
+
+    for j in (1, 2, 3):
+        copy(gps.at[0], gpr.at[j - 1], p_send + j - 1, p_recv + j - 1, zpeer(j)).wait_recv()
+    pooled_back = gps[z].astype(f32)
+    for j in range(3):
+        pooled_back = pooled_back + gpr[j].astype(f32)
+    count = cnt[z]
+    pieces = [pooled_back[:, 128 * chunk:128 * chunk + 128] / count for chunk in range(4)]
+    high, low = halves(jnp.concatenate(pieces, 1))
+    fg[...] = dot(mt[z], high, ROWS_T) + dot(mt[z], low, ROWS_T)
+    ok = val[z]
+
+    @pl.when(z > 0)
+    def _():
+        ru_copy(2).wait_recv()
+        dxf[z] = dxf[z] + rxu[2].astype(f32)
+
+    @pl.when(z < 3)
+    def _():
+        rd_copy(2).wait_recv()
+        dxf[z] = dxf[z] + rxd[2].astype(f32)
+
+    for chunk in range(4):
+        cols = slice(128 * chunk, 128 * chunk + 128)
+        fg[:, cols] = fg[:, cols] + dxf[z, :, cols] * ok
+    q_send, q_recv = names.take(8), names.take(8)
+
+    def fg_copy(n):
+        dev, _ = peer(*plane[n])
+        rows = pl.ds(pl.multiple_of(256 * dev["wa"] + 64 * dev["ha"], 64), 64)
+        return copy(fg.at[rows, :], fgrad_out.at[w, :, pl.ds(g512, 512)], q_send + n, q_recv + n, dev)
+
+    for n in range(7):
+        fg_copy(n).start()
+    fg_own = pltpu.make_async_copy(
+        fg.at[pl.ds(own_row, 64), :], fgrad_out.at[w, :, pl.ds(g512, 512)], sems.at[q_send + 7]
+    )
+    fg_own.start()
+
+    for n, (kx, ky) in enumerate(chips):
+        dev, block = peer(kx, ky, 0)
+        copy(bgh, bga_of(block, w), bx_send + n, bx_recv + n, dev).wait_recv()
+        bg_core(n, block).start()
+
+    for n in range(7):
+        small_copy(n).wait_recv()
+    total = small[...]
+    for n in range(7):
+        total = total + smr[n]
+    small_out[0:48, :] = total[0:48]
+    small_out[48:56, :] = total[48:56]
+    for kx, ky in [(0, 0)] + chips:
+        dev, block = peer(kx, ky, 0)
+        mine = small[...] if kx + ky == 0 else smr[plane.index((kx, ky, 0))]
+        both = mine + smr[plane.index((kx, ky, 1))]
+        small_out[pl.ds(56 + block, 1), :] = both[50:51]
+        small_out[pl.ds(60 + block, 1), :] = both[51:52]
+
+    logits_other = copy(lts.at[1 - w], lts.at[1 - w], ls_send, ls_recv, peer(0, 0, 1)[0])
+    logits_other.wait_recv()
+    logits_out[...] = lts[...]
+
+    for n, (kx, ky) in enumerate([*chips, (0, 0)]):
+        block = peer(kx, ky, 0)[1]
+        copy(bga_of(block, 1 - w), bga_of(block, 1 - w), by_send + n, by_recv + n, peer(0, 0, 1)[0]).wait_recv()
+    out_sem = names.take()
+    bg_out = pltpu.make_async_copy(bga, bgrad_out, sems.at[out_sem])
+    bg_out.start()
+
+    for n in range(7):
+        dev, block = peer(*plane[n])
+        copy(
+            fg.at[pl.ds(0, 64), :],
+            fgrad_out.at[dev["wa"], :, pl.ds(pl.multiple_of(512 * block, 512), 512)],
+            q_send + n, q_recv + n, dev,
+        ).wait_recv()
+    fg_own.wait()
+
+    @pl.when(w == yq)
+    def _():
+        for t in range(TAPS):
+            tap_own(t).wait()
+
+    @pl.when(w != yq)
+    def _():
+        for t in range(TAPS):
+            tap_copy(t).wait()
+
+    for c in a_copies:
+        c.wait_send()
+    seed_copy.wait_send()
+    for k in range(3):
+        pl.when((z >= k) & (z < 3))(lambda: up_copy(k).wait_send())
+        pl.when((z + k <= 3) & (z > 0))(lambda: dn_copy(k).wait_send())
+        pl.when(up_on(k))(lambda: ru_copy(k).wait_send())
+        pl.when(dn_on(k))(lambda: rd_copy(k).wait_send())
+    for j in (1, 2, 3):
+        copy(sd.at[z], sd.at[z], sz_send + j - 1, sz_recv + j - 1, zpeer(j)).wait_send()
+        copy(bos, share(bo, z), f_send + j - 1, f_recv + j - 1, zpeer(j)).wait_send()
+        copy(lt.at[0], ltr.at[j - 1], lt_send + j - 1, lt_recv + j - 1, zpeer(j)).wait_send()
+        copy(gps.at[0], gpr.at[j - 1], p_send + j - 1, p_recv + j - 1, zpeer(j)).wait_send()
+    for level in range(4):
+        for c in range(4):
+            to_level_owner(level, lambda kx, ky: pre_copy(level, c, kx, ky).wait_send())
+
+        @pl.when(g == level)
+        def _():
+            for j in (1, 2, 3):
+                copy(
+                    gb.at[:, pl.ds(0, SPANS[level]), pl.ds(0, 128)],
+                    grr.at[j - 1, :, pl.ds(0, SPANS[level]), :],
+                    n_send + j - 1, n_recv + j - 1, zpeer(j),
+                ).wait_send()
+            for kx, ky in chips:
+                slot = kx + 2 * ky - 1
+                copy(
+                    gpre.at[:, pl.ds(0, SPANS[level]), :], gpa.at[:, pl.ds(STARTS[level], SPANS[level]), :],
+                    o_send + slot, o_recv + 3 * level + slot, peer(kx, ky, 0)[0],
+                ).wait_send()
+    for kx, ky in chips:
+        for c in range(4):
+            conv_copy(c, kx, ky).wait_send()
+        for stage in range(2):
+            stat_copy(stage, kx, ky).wait_send()
+        gc_copy(kx, ky, q).wait_send()
+        bg_chip(kx, ky).wait_send()
+    dw_copy.wait_send()
+    bg_copy.wait_send()
+    logits_copy.wait_send()
+    for n in range(7):
+        small_copy(n).wait_send()
+        fg_copy(n).wait_send()
+    for n in range(4):
+        bg_core(n, g).wait_send()
+    bg_out.wait()
+    assert names.count <= SEMAPHORES
+
+
+SEMAPHORES = 256
+
+
+def canvas_body(
+    mesh, features, region_boxes, branch_weight, branch_gain, branch_bias, conv_weight, norm_gain, norm_bias,
+    class_weight, class_bias, cotangent,
+):
+    f32, bf16 = jnp.float32, jnp.bfloat16
+    micros, tile_rows, tile_cols, channels = features.shape
+    pixels = tile_rows * tile_cols
+    classes = class_bias.shape[0]
+    z, w = lax.axis_index("col"), lax.axis_index("wa")
+    own_boxes = lax.dynamic_slice_in_dim(region_boxes, micros * z, micros, 0)
+    at = jnp.arange(pixels, dtype=jnp.int32)
+    y = (lax.axis_index("ha") * tile_rows + at // tile_cols)[None, None]
+    xx = (w * tile_cols + at % tile_cols)[None, None]
+    top, left, bottom, right = [own_boxes[:, :, e, None] for e in range(4)]
+    valid = jnp.any((y >= top) & (y < bottom) & (xx >= left) & (xx < right), 1).astype(f32)
+    seeds = jnp.transpose((cotangent.reshape(micros, pixels, classes) * valid[:, :, None]), (0, 2, 1))
+    seeds = jnp.pad(seeds, ((0, 0), (0, 24 - classes), (0, 0)))
+    blank = jnp.zeros_like(seeds)
+    seeds = jnp.where(w == 0, jnp.concatenate([seeds, blank], 2), jnp.concatenate([blank, seeds], 2))
+    cwt = jnp.pad(class_weight.T, ((0, 24 - classes), (0, 0)))
+    lane_table, row_table = bin_tables()
+
+    vmem = pl.BlockSpec(memory_space=pltpu.VMEM)
+    hbm = pl.BlockSpec(memory_space=pl.ANY)
+    smem = pl.BlockSpec(memory_space=pltpu.SMEM)
+    V = pltpu.VMEM
+    scratch = [
+        V((4, 512, 512), bf16),
+        V((4, 512, 512), bf16),
+        V((1024, 1152), bf16),
+        V((4, 512, 128), bf16),
+        V((4, 512, 128), bf16),
+        V((4, 512, 128), bf16),
+        V((4, BINS, 512), bf16),
+        V((4, BINS, 128), f32),
+        V((4, BINS, 512), bf16),
+        V((4, BINS, 128), f32),
+        V((3, 4, WIDE, 128), f32),
+        V((4, WIDE, 128), bf16),
+        V((4, 128, 512), bf16),
+        V((4, 512, 128), f32),
+        V((2, 272, 1152), f32),
+        V((4, 2, 256, 128), f32),
+        V((3, 4, 2, 64, 128), f32),
+        V((4, 2, 256, 128), bf16),
+        V((4, 512, 1152), bf16),
+        V((3, 2, 272, 128), f32),
+        V((4, 512, 512), f32),
+        V((3, 512, 512), bf16),
+        V((3, 512, 512), bf16),
+        V((3, 512, 512), bf16),
+        V((3, 512, 512), bf16),
+        V((4, WIDE, 512), bf16),
+        V((3, 4, WIDE, 128), bf16),
+        V((4, WIDE, 128), f32),
+        V((4, BINS, 128), f32),
+        V((4, BINS, 512), bf16),
+        V((3, BINS, 512), bf16),
+        V((2, 512, 1152), f32),
+        V((512, 1152), f32),
+        V((4, 512, 128), f32),
+        V((4, 256, 128), f32),
+        V((4, 256, 128), bf16),
+        V((1, 24, 128), f32),
+        V((4, 24, 128), f32),
+        V((4, 24, 128), f32),
+        V((3, 24, 128), f32),
+        V((2, 24, 128), f32),
+        V((2, 8, 128), f32),
+        V((2, 3, 8, 128), f32),
+        V((56, 128), f32),
+        V((7, 56, 128), f32),
+        V((4, WIDE, 128), f32),
+        V((4, WIDE, 128), f32),
+        V((2, 512, 128), f32),
+        V((4, channels, 128), bf16),
+        V((512, 512), f32),
+        pltpu.SemaphoreType.DMA((SEMAPHORES,)),
+    ]
+    share = conv_weight.shape[2]
+    logits_t, feature_grad, branch_grad, small, conv_grad = pl.pallas_call(
+        head_kernel,
+        out_shape=(
+            jax.ShapeDtypeStruct((2, 24, 128), f32),
+            jax.ShapeDtypeStruct((micros, pixels, channels), f32),
+            jax.ShapeDtypeStruct((4, channels, share), bf16),
+            jax.ShapeDtypeStruct((64, 128), f32),
+            jax.ShapeDtypeStruct((TAPS, 512, share), f32),
+        ),
+        in_specs=[smem, vmem, vmem, hbm, vmem, hbm, hbm, vmem, vmem, vmem, vmem, vmem],
+        out_specs=(vmem, hbm, hbm, vmem, hbm),
+        scratch_shapes=scratch,
+        compiler_params=pltpu.CompilerParams(
+            collective_id=0, has_side_effects=True, vmem_limit_bytes=60 * 2**20
+        ),
+    )(
+        region_boxes.reshape(-1), lane_table, row_table, features.reshape(micros, pixels, channels), seeds,
+        conv_weight, branch_weight, branch_gain, branch_bias, norm_gain.reshape(1, -1), norm_bias.reshape(1, -1), cwt,
+    )
+    tile = lax.dynamic_slice_in_dim(logits_t, w * pixels, pixels, 2)[:, :classes]
+    logits = (jnp.transpose(tile, (0, 2, 1)) + class_bias) * valid[:, :, None]
+    return (
+        logits.reshape(micros, tile_rows, tile_cols, classes),
+        feature_grad.reshape(features.shape),
+        branch_grad.astype(f32),
+        small[56:60],
+        small[60:64],
+        conv_grad,
+        small[49],
+        small[48],
+        small[:classes].T,
+        small[24:24 + classes, 0],
+    )
 
 
 def extended(block, sides, width):
@@ -86,7 +1044,7 @@
     return logistic * (1.0 + inputs * (1.0 - logistic))
 
 
-def body(
+def tiled_body(
     features,
     region_boxes,
     branch_weight,
@@ -361,7 +1319,7 @@
         P("col", "ha", "wa", None),
     )
     return jax.shard_map(
-        body,
+        functools.partial(canvas_body, mesh) if whole_canvas_plan(mesh) else tiled_body,
         mesh=mesh,
         in_specs=placed,
         out_specs=(

time: 929 us -> 190 us (0.20)
  waiting for transfers between devices: 503 us -> 0 us
  Pallas kernels: 0 us -> 167 us
  matrix products: 124 us -> 0 us
  blocking collectives: 96.8 us -> 0 us
  other arithmetic: 83 us -> 5.65 us
  local copies, waits for them, and re-layouts: 55.6 us -> 13.3 us
  starting transfers between devices: 35.5 us -> 0 us
  between operations: 20.7 us -> 0.7 us
    reduce_scatter x7 -> x0, waiting for transfers between devices: 211 us -> none  [the longest x1 128 us: body(): lax.psum_scatter(conv_total.reshape(9, -1, share), ('ha', 'wa'), scatter_...]
    psum x2 -> x0, waiting for transfers between devices: 200 us -> none  [the longest x1 148 us: body(): bin_grad = lax.psum(bin_local, ('ha', 'wa', 'col'))]
    pallas_call x0 -> x1, Pallas kernels: none -> 167 us  [canvas_body(): pl.pallas_call(head_kernel, out_shape=(jax.ShapeDtypeStruct((2, 24, 128),...]
    dot_general x56 -> x0, matrix products: 124 us -> none  [the longest x2 34.6 us: body(): jnp.einsum('pk,pe->ke', columns, grad_low, preferred_element_type=jnp.flo...]
    all_gather x4 -> x0, waiting for transfers between devices: 87.4 us -> none  [the longest x2 87.4 us: body(): pooled_all = lax.all_gather(pooled[None], 'col', axis=0, tiled=True)]
    all_gather x4 -> x0, blocking collectives: 58.5 us -> none  [the longest x2 31.6 us: body(): branch_full = lax.all_gather(branch_local, 'col', axis=2, tiled=True)]
    psum x2 -> x0, blocking collectives: 38.4 us -> none  [the longest x1 22.9 us: body(): lax.psum((jnp.sum(grad_affine, 0), jnp.sum(grad_affine * normed, 0), jnp....]
    ppermute x16 -> x0, starting transfers between devices: 34.5 us -> none  [the longest x8 24.2 us: extended(): lax.ppermute(lax.slice_in_dim(block, block.shape[dim] - width, None, axis...]
  transfers between devices with their start and end apart: 29 -> 0, of which waited for: 10 -> 0; matrix products, arithmetic and copies ran while one was open for 18% -> 0% of each run, Pallas kernels for 0% -> 0%
where the time goes in v1:
time: 190 us; the launch traced here: 186 us
  Pallas kernels  167 us (88%)
  local copies, waits for them, and re-layouts  13.3 us (7%)
  other arithmetic  5.65 us (3%)
    pallas_call x1, Pallas kernels, canvas_body(): pl.pallas_call(head_kernel, out_shape=(jax.ShapeDtypeStruct((2, 24, 128),...  167 us
    convert_element_type x1, other arithmetic, canvas_body(): branch_grad.astype(f32)  4.02 us

profile of v1, /device:TPU:8, one launch (start us, length us, event | category | flops | bytes accessed | tf_op | source)
XLA Modules:
  0.0 186.5 jit_solution(2221619108967789109)
XLA Ops:
  0.7 0.9 constant_dynamic-slice_fusion.2
  1.6 0.1 copy.38
  1.7 0.1 copy.40
  1.8 0.1 copy.39
  1.9 0.1 copy.41
  2.0 0.1 and_reduce_fusion
  2.1 1.3 pad.11.cwt
  3.4 0.8 copy.37
  4.2 0.6 reshape.69.boxes
  4.8 0.9 copy.42
  5.7 0.7 pad_select_fusion.seeds
  6.4 0.0 copy-start.2
  6.4 166.8 %shard_map.204 = (f32[2,24,128]{2,1,0:T(8,128)}, f32[2,64,2048]{2,1,0:T(8,128)}, bf16[4,2048,128]{2,1,0:T(8,128)(2,1)}, f32[64,128]{1,0:T(8,128)}, f32[9,512,128]{2,1,0:T(8,128)}) custom-call(s32[96]{0:T(128)} %reshape.69.boxes, f32[4,8,128]{2,1,0:T(8,128)} %constant.59.clone.lane_table, f32[5,176,128]{2,1,0:T(8,128)} %constant.60.clone.row_table, ...), custom_call_target="tpu_custom_call" | custom-call | tf_op jit(solution)/shard_map/pallas_call | solution.py:934
  173.3 0.0 copy-done.2
  173.3 0.8 fusion.1
  174.1 1.3 slice_reduce_fusion
  175.4 1.3 slice_bitcast_fusion.1
  176.7 1.3 fusion.4
  178.0 1.3 slice_bitcast_fusion
  179.3 0.7 copy.43
  180.1 0.0 copy-start.1
  180.1 0.0 copy-start
  180.1 4.0 %convert_element_type.15 = f32[4,2048,128]{2,1,0:T(8,128)} convert(bf16[4,2048,128]{2,1,0:T(8,128)(2,1)} %get-tuple-element.17) | non-fusion elementwise | flops 1048576 | bytes 6291456 | tf_op jit(solution)/shard_map/convert_element_type | solution.py:958
  184.1 0.0 copy-done.1
  184.1 1.0 copy.46
  185.1 0.0 copy-done
  185.1 1.4 copy.47
  (4 shorter events, 0.0 us)
Async XLA Ops:
  6.4 166.8 %copy-start.2 = (f32[19]{0:T(128)S(1)}, f32[19]{0:T(128)}, u32[]{:S(2)}) copy-start(f32[19]{0:T(128)} %param.22) | copy-start | bytes 232
  180.1 4.0 %copy-start.1 = (f32[2,64,2048]{2,1,0:T(8,128)S(1)}, f32[2,64,2048]{2,1,0:T(8,128)}, u32[]{:S(2)}) copy-start(f32[2,64,2048]{2,1,0:T(8,128)} %get-tuple-element.16) | copy-start | bytes 3145732
  180.1 5.0 %copy-start = (f32[9,512,128]{2,1,0:T(8,128)S(1)}, f32[9,512,128]{2,1,0:T(8,128)}, u32[]{:S(2)}) copy-start(f32[9,512,128]{2,1,0:T(8,128)} %get-tuple-element.55) | copy-start | bytes 7077892

commit v2 on v1

--- a/solution.py
+++ b/solution.py
@@ -27,8 +27,8 @@
 
 def bin_tables():
     lanes = np.zeros((4, 8, 128), np.float32)
-    rows = np.zeros((5, BINS, 128), np.float32)
-    rows[3] = 1.0
+    rows = np.zeros((BINS, 8), np.float32)
+    rows[:, 3] = 1.0
     for level, n in enumerate(LEVELS):
         lanes[level, 3, :] = n - 1
         for k in range(3):
@@ -39,7 +39,7 @@
                     lanes[level, 4, b] = 1.0
                     row = STARTS[level] + b
                     for at, value in enumerate((k, i, j, n, 1.0)):
-                        rows[at, row] = value
+                        rows[row, at] = value
     return lanes, rows
 
 
@@ -71,20 +71,33 @@
 
 
 def head_kernel(
-    boxes, lane_table, row_table, feat, seeds, wconv, wbranch, bgain, bbias, ngain, nbias, cwt,
+    boxes, lane_table, row_table, feat, cot, wconv, wbranch, bgain, bbias, ngain, nbias, cw_in, cb,
     logits_out, fgrad_out, bgrad_out, small_out, cgrad_out,
-    x, lv, wall, wb, uh, ul, mt, cnt, po, pre, prr, bos, bo, val, yp, p, cr, gc, g9, gp3,
-    dxf, sbu, sbd, rxu, rxd, gb, grr, gpre, gpa, gps, gpr, dw, dwr, bg, bgr, bgh, seed_in, sd, lt, ltr, lts,
-    st, str_, small, smr, nb_s, af_s, cn_s, bga, fg, sems,
+    x, lv, wall, wb2, u2, ut, mt, cnt, po, pre, prr, bos, bor, bo2, val, yp, p, cr, gc, g9, gp3, tb,
+    dxf, sbu, sbd, rxu, rxd, gb, grr, gpre, gpa, gpx, gps, gpr, dw, dwr, bg, bgr, bgh, seed_in, sd, lt, ltr, lts,
+    st, str_, small, smr, nb_s, af_s, cn_s, bga, fg, fgh, cwt, seeds, square, dwh, dwx, bi_s, sems, turn,
 ):
     f32, bf16 = jnp.float32, jnp.bfloat16
     q, w, z = lax.axis_index("ha"), lax.axis_index("wa"), lax.axis_index("col")
     xq, yq = lax.rem(q, 2), lax.div(q, 2)
     g = 2 * xq + yq
+    classes = cb.shape[1]
     zm = lax.div(z, 2)
     zz = z * (1 - zm) + (3 - z) * zm
     names = Sems()
-    later = []
+    finals = []
+    due = {}
+
+    def arrive(name):
+        due.pop(name)()
+
+    def each(copies, method):
+        def run():
+            for c in copies:
+                getattr(c, method)()
+
+        return run
+
 
     def peer(kx, ky, kw):
         px = xq + kx - 2 * kx * xq
@@ -101,6 +114,12 @@
 
     plane = [(kx, ky, kw) for kw in (0, 1) for ky in (0, 1) for kx in (0, 1) if kx + ky + kw]
     chips = [(1, 0), (0, 1), (1, 1)]
+
+    barrier = pltpu.get_barrier_semaphore()
+    for kx, ky, kw in plane:
+        pl.semaphore_signal(barrier, 1, device_id=peer(kx, ky, kw)[0], device_id_type=MESH)
+    for j in (1, 2, 3):
+        pl.semaphore_signal(barrier, 1, device_id=zpeer(j), device_id_type=MESH)
 
     g512 = pl.multiple_of(g * 512, 512)
     weight_copies = []
@@ -114,55 +133,77 @@
                     sems.at[s],
                 )
             )
-    s = names.take()
-    weight_copies.append(pltpu.make_async_copy(wbranch.at[:, pl.ds(g512, 512), :], wb, sems.at[s]))
+    for twice in range(2):
+        s = names.take()
+        weight_copies.append(
+            pltpu.make_async_copy(
+                wbranch.at[:, pl.ds(g512, 512), :], wb2.at[:, :, pl.ds(128 * twice, 128)], sems.at[s]
+            )
+        )
     for c in weight_copies:
         c.start()
-
-    prr[...] = jnp.zeros(prr.shape, f32)
-    grr[...] = jnp.zeros(grr.shape, bf16)
-    bo[...] = jnp.zeros(bo.shape, bf16)
+    due["weights"] = each(weight_copies, "wait")
+
+    for half in range(2):
+        bo2[:, 128 * half + WIDE:128 * half + 128, :] = jnp.zeros((4, 128 - WIDE, 512), bf16)
     yp[:, 0:8, :] = jnp.zeros((2, 8, 1152), f32)
     yp[:, 264:272, :] = jnp.zeros((2, 8, 1152), f32)
     gp3[:, :, 0:8, :] = jnp.zeros((3, 2, 8, 128), f32)
     gp3[:, :, 264:272, :] = jnp.zeros((3, 2, 8, 128), f32)
     small[...] = jnp.zeros(small.shape, f32)
     st[...] = jnp.zeros(st.shape, f32)
-
-    barrier = pltpu.get_barrier_semaphore()
-    for kx, ky, kw in plane:
-        pl.semaphore_signal(barrier, 1, device_id=peer(kx, ky, kw)[0], device_id_type=MESH)
-    for j in (1, 2, 3):
-        pl.semaphore_signal(barrier, 1, device_id=zpeer(j), device_id_type=MESH)
+    p[...] = jnp.zeros(p.shape, f32)
+    nb_s[...] = jnp.zeros(nb_s.shape, f32)
+    gpre[...] = jnp.zeros(gpre.shape, f32)
+    cwt[...] = jnp.zeros(cwt.shape, f32)
+    cwt[0:classes, :] = cw_in[...]
     pl.semaphore_wait(barrier, 10)
 
     q64 = pl.multiple_of(64 * q, 64)
     a_send, a_recv = names.take(8), names.take(8)
-    a_copies = []
     own_row = pl.multiple_of(256 * w + 64 * q, 64)
-    for n, (kx, ky, kw) in enumerate(plane):
-        dev, block = peer(kx, ky, kw)
-        c = copy(
-            feat.at[dev["wa"], :, pl.ds(pl.multiple_of(512 * block, 512), 512)],
-            x.at[z, pl.ds(own_row, 64), :],
-            a_send + n, a_recv + n, dev,
+    own = pltpu.make_async_copy(feat.at[w, :, pl.ds(g512, 512)], x.at[z, pl.ds(own_row, 64), :], sems.at[a_send])
+
+    def tile_copy(t, kx, ky):
+        n = 4 * (t + w - 2 * t * w) + 2 * ky + kx
+        dev, block = peer(kx, ky, 0)
+        return copy(
+            feat.at[t, :, pl.ds(pl.multiple_of(512 * block, 512), 512)], x.at[z, pl.ds(own_row, 64), :],
+            a_send + n, a_recv + n, {"ha": dev["ha"], "wa": t},
         )
-        c.start()
-        a_copies.append(c)
-    own = pltpu.make_async_copy(feat.at[w, :, pl.ds(g512, 512)], x.at[z, pl.ds(own_row, 64), :], sems.at[a_send + 7])
+
+    def tiles(t, method):
+        for kx, ky in chips:
+            getattr(tile_copy(t, kx, ky), method)()
+        pl.when(w != t)(lambda: getattr(tile_copy(t, 0, 0), method)())
+
+    def tiles_wait():
+        for n, (kx, ky, kw) in enumerate(plane):
+            at = 4 * kw + 2 * ky + kx
+            copy(
+                feat.at[0, :, pl.ds(0, 512)], x.at[z, pl.ds(own_row, 64), :], a_send + at, a_recv + at, peer(kx, ky, kw)[0]
+            ).wait_recv()
+
     own.start()
-    sc_send, sc_recv = names.take(), names.take()
-    seed_copy = copy(seeds.at[1 - w], seed_in.at[0], sc_send, sc_recv, peer(0, 0, 1)[0])
-    seed_copy.start()
-
-    def scalars(canvas):
-        index = 2 * canvas + w
-        return [[boxes[index * 12 + 4 * k + e] for k in range(3)] for e in range(4)]
+    tiles(0, "start")
+
+    def scalars(canvas, micro=None):
+        index = 2 * canvas + (w if micro is None else micro)
+        return [[boxes[k, e, index] for k in range(3)] for e in range(4)]
 
     def px(rows, lanes, axis, start=0):
         at = lax.broadcasted_iota(jnp.int32, (rows, lanes), axis) + start
         half = at // 256
         return (at // 8 % 32).astype(f32), (half * 8 + at % 8).astype(f32)
+
+    def tile_valid(micro):
+        at = lax.broadcasted_iota(jnp.int32, (64, 128), 0)
+        y, xx = (8 * q + at // 8).astype(f32), (8 * w + at % 8).astype(f32)
+        top, left, bottom, right = [[v.astype(f32) for v in values] for values in scalars(z, micro)]
+        ok = jnp.zeros((64, 128), f32)
+        for k in range(3):
+            ok = jnp.where((y >= top[k]) & (y < bottom[k]) & (xx >= left[k]) & (xx < right[k]), 1.0, ok)
+        return ok
 
     def layout(c):
         top, left, bottom, right = [[v.astype(f32) for v in values] for values in scalars(c)]
@@ -180,9 +221,12 @@
         inside = (y >= t_) & (y < b_) & (xx >= l_) & (xx < r_) & (real > 0.0)
         weights = jnp.where(inside, rw * cw, 0.0)
         high, low = halves(weights)
-        uh[c] = high
-        ul[c] = low
-        box, bi, bj, n, real = [row_table[e] for e in range(5)]
+        u2[c, :, 0:128] = high
+        u2[c, :, 128:256] = low
+        high, low = halves(weights.T)
+        ut[c, 0:128, :] = high
+        ut[c, 128:256, :] = low
+        box, bi, bj, n, real = [jnp.broadcast_to(row_table[:, e:e + 1], (BINS, 128)) for e in range(5)]
         t_, l_, b_, r_ = [pick3(box, v) for v in (top, left, bottom, right)]
         h, wd = b_ - t_, r_ - l_
         row_low = jnp.floor((bi * h + 0.5) / n)
@@ -236,122 +280,216 @@
             wanted = (xq + kx - 2 * kx * xq == lx) & (yq + ky - 2 * ky * yq == ly)
             pl.when(wanted)(functools.partial(action, kx, ky))
 
-    def process(c):
-        po_sum = dot(mt[c], x[c])
+    def pool(c):
+        total = dot(mt[c], x[c])
         for chunk in range(4):
-            po[c, :, 128 * chunk:128 * chunk + 128] = (po_sum[:, 128 * chunk:128 * chunk + 128] / cnt[c]).astype(bf16)
+            cols = slice(128 * chunk, 128 * chunk + 128)
+            po[c, :, cols] = (total[:, cols] / cnt[c]).astype(bf16)
+
+    def branch_products(c):
         for level in range(4):
             rows = slice(STARTS[level], STARTS[level] + SPANS[level])
-            pre[c, rows, :] = dot(po[c, rows, :], wb[level])
+            pre[c, rows, :] = dot(po[c, rows, :], wb2[level, :, 0:128])
         for level in range(4):
             to_level_owner(level, lambda kx, ky, level=level: pre_copy(level, c, kx, ky).start())
-        out0, out1 = conv_part(x[c], 0)
-        p[c, 0] = out0
-        p[c, 1] = out1
-
-    for c in range(4):
-        layout(c)
-
-    for c in weight_copies:
-        c.wait()
-    for c in a_copies:
-        c.wait_recv()
-    own.wait()
+
+    def conv_add(c, operand, part):
+        out0, out1 = conv_part(operand, part)
+        p[c, 0] = p[c, 0] + out0
+        p[c, 1] = p[c, 1] + out1
+
+    layout(z)
+    for copy_out in (tiles,):
+        copy_out(0, "wait_send")
+        copy_out(1, "start")
+    due["A"] = tiles_wait
+    due["A own"] = own.wait
+    finals.append(lambda: tiles(1, "wait_send"))
+
+    w64 = pl.multiple_of(64 * w, 64)
+    square[...] = jnp.zeros(square.shape, f32)
+    for micro in range(2):
+        square[pl.ds(w64, 64), 0:classes] = cot[micro] * tile_valid(micro)[:, 0:classes]
+        seeds[micro] = square[...].T[0:24]
+    sc_send, sc_recv = names.take(), names.take()
+    seed_copy = copy(seeds.at[1 - w], seed_in.at[0], sc_send, sc_recv, peer(0, 0, 1)[0])
+    seed_copy.start()
+    due["seed"] = seed_copy.wait_recv
+    finals.append(seed_copy.wait_send)
+
+    arrive("weights")
+    arrive("A")
+    arrive("A own")
     ok = val[z]
     for chunk in range(4):
         cols = slice(128 * chunk, 128 * chunk + 128)
         x[z, :, cols] = (x[z, :, cols].astype(f32) * ok).astype(bf16)
 
-    up_send, up_recv, dn_send, dn_recv = names.take(3), names.take(3), names.take(3), names.take(3)
-
-    def up_copy(k):
-        return copy(x.at[z - k], x.at[z - k], up_send + k, up_recv + k, {"col": z + 1})
-
-    def dn_copy(k):
-        return copy(x.at[z + k], x.at[z + k], dn_send + k, dn_recv + k, {"col": z - 1})
-
-    def up_wait(k):
-        copy(x.at[z - k], x.at[z - k], up_send + k - 1, up_recv + k - 1, {"col": z}).wait_recv()
-
-    def dn_wait(k):
-        copy(x.at[z + k], x.at[z + k], dn_send + k - 1, dn_recv + k - 1, {"col": z}).wait_recv()
-
-    pl.when(z < 3)(lambda: up_copy(0).start())
-    pl.when(z > 0)(lambda: dn_copy(0).start())
-
-    seed_copy.wait_recv()
+    up_send, up_recv, dn_send, dn_recv = names.take(6), names.take(6), names.take(6), names.take(6)
+
+    def half_of(c, h):
+        return x.at[c, pl.ds(256 * h, 256), :]
+
+    def up_copy(k, h):
+        part = half_of(z - k, h)
+        return copy(part, part, up_send + 2 * k + h, up_recv + 2 * k + h, {"col": z + 1})
+
+    def dn_copy(k, h):
+        part = half_of(z + k, h)
+        return copy(part, part, dn_send + 2 * k + h, dn_recv + 2 * k + h, {"col": z - 1})
+
+    def take_in(k, h):
+        n = 2 * (k - 1) + h
+
+        @pl.when(z >= k)
+        def _():
+            part = half_of(z - k, h)
+            copy(part, part, up_send + n, up_recv + n, {"col": z}).wait_recv()
+
+        @pl.when(z + k <= 3)
+        def _():
+            part = half_of(z + k, h)
+            copy(part, part, dn_send + n, dn_recv + n, {"col": z}).wait_recv()
+
+    other = peer(0, 0, 1)[0]
+
+    def up_last(k):
+        return (w == 0) & (z < 3) & (z == k)
+
+    def dn_last(k):
+        return (w == 0) & (z > 0) & (3 - z == k)
+
+    def pass_on(k, h):
+        pl.when((z >= k) & (z < 3))(lambda: up_copy(k, h).start())
+        pl.when((z + k <= 3) & (z > 0))(lambda: dn_copy(k, h).start())
+        if k == 2 and h == 1:
+            give_turn(k)
+
+    def passed_on():
+        for k in range(3):
+            for h in range(2):
+                up_done, dn_done = (z >= k) & (z < 3), (z + k <= 3) & (z > 0)
+                if h == 0 and k < 2:
+                    up_done = up_done & jnp.logical_not(up_last(k))
+                    dn_done = dn_done & jnp.logical_not(dn_last(k))
+                pl.when(up_done)(lambda: up_copy(k, h).wait_send())
+                pl.when(dn_done)(lambda: dn_copy(k, h).wait_send())
+
+    finals.append(passed_on)
+
+    def give_turn(k):
+        @pl.when(up_last(k))
+        def _():
+            if k < 2:
+                up_copy(k, 0).wait_send()
+            pl.semaphore_signal(turn.at[0], 1, device_id=other, device_id_type=MESH)
+
+        @pl.when(dn_last(k))
+        def _():
+            if k < 2:
+                dn_copy(k, 0).wait_send()
+            pl.semaphore_signal(turn.at[1], 1, device_id=other, device_id_type=MESH)
+
+    def own_turn(up):
+        def start():
+            pl.semaphore_wait(turn.at[0 if up else 1], 1)
+            for h in range(2):
+                (up_copy(0, h) if up else dn_copy(0, h)).start()
+
+        pl.when((z < 3) if up else (z > 0))(start)
+
+    pool(z)
+    h_send, h_recv = names.take(3), names.take(3)
+    po_copies = [copy(po.at[z], po.at[z], h_send + j - 1, h_recv + j - 1, zpeer(j)) for j in (1, 2, 3)]
+
+    @pl.when(w == 0)
+    def _():
+        each(po_copies, "start")()
+        pass_on(0, 0)
+        pass_on(0, 1)
+
+    finals.append(lambda: pl.when(w == 0)(each(po_copies, "wait_send")))
+
+    arrive("seed")
     sd[z] = seeds[w] + seed_in[0]
     sz_send, sz_recv = names.take(3), names.take(3)
-    for j in (1, 2, 3):
-        copy(sd.at[z], sd.at[z], sz_send + j - 1, sz_recv + j - 1, zpeer(j)).start()
-
-    process(z)
-    for k in (1, 2, 3):
-
-        @pl.when(z >= k)
-        def _():
-            up_wait(k)
-            if k < 3:
-                pl.when(z < 3)(lambda: up_copy(k).start())
-
-        @pl.when(z + k <= 3)
-        def _():
-            dn_wait(k)
-            if k < 3:
-                pl.when(z > 0)(lambda: dn_copy(k).start())
-
-        pl.when(z >= k)(lambda: process(z - k))
-        pl.when(z + k <= 3)(lambda: process(z + k))
-
-    for c in range(4):
-        for kx, ky in chips:
-            slot = kx + 2 * ky - 1
-            for level in range(4):
-
-                @pl.when(g == level)
-                def _():
-                    copy(
-                        pre.at[c, pl.ds(STARTS[level], SPANS[level]), :],
-                        prr.at[slot, c, pl.ds(0, SPANS[level]), :],
-                        e_send, e_recv + 4 * slot + c, peer(0, 0, 1)[0],
-                    ).wait_recv()
-
-    nb_s[...] = jnp.zeros(nb_s.shape, f32)
-    for level in range(4):
-
-        @pl.when(g == level)
-        def _():
+    sd_copies = [copy(sd.at[z], sd.at[z], sz_send + j - 1, sz_recv + j - 1, zpeer(j)) for j in (1, 2, 3)]
+    each(sd_copies, "start")()
+    finals.append(each(sd_copies, "wait_send"))
+
+    def sd_wait():
+        for j in (1, 2, 3):
+            src = lax.rem(z + 4 - j, 4)
+            copy(sd.at[src], sd.at[src], sz_send + j - 1, sz_recv + j - 1, zpeer(j)).wait_recv()
+
+    due["sd"] = sd_wait
+
+    branch_products(z)
+    conv_add(z, x[z], 0)
+
+    def rest(i, carry):
+        layout(lax.rem(z + i, 4))
+        return carry
+
+    lax.fori_loop(1, 4, rest, 0)
+
+    def pre_wait():
+        for c in range(4):
+            for kx, ky in chips:
+                slot = kx + 2 * ky - 1
+                for level in range(4):
+
+                    @pl.when(g == level)
+                    def _():
+                        copy(
+                            pre.at[c, pl.ds(STARTS[level], SPANS[level]), :],
+                            prr.at[slot, c, pl.ds(0, SPANS[level]), :],
+                            e_send, e_recv + 4 * slot + c, peer(0, 0, 1)[0],
+                        ).wait_recv()
+
+    def pre_sent():
+        for level in range(4):
             for c in range(4):
-                nb_s[c, 0:SPANS[level], :] = pre[c, STARTS[level]:STARTS[level] + SPANS[level], :]
-
+                to_level_owner(level, lambda kx, ky: pre_copy(level, c, kx, ky).wait_send())
+
+    finals.append(pre_sent)
     level_n = jnp.where(g == 0, 1.0, jnp.where(g == 1, 2.0, jnp.where(g == 2, 3.0, 6.0)))
     samples = 12.0 * level_n * level_n
 
     def rows_of(value):
         return value.reshape(4 * WIDE, 128)
 
-    pre_all = rows_of(nb_s[...] + prr[0] + prr[1] + prr[2])
-    average = jnp.sum(pre_all, 0, keepdims=True) / samples
-    spread = jnp.sum(pre_all * pre_all, 0, keepdims=True) / samples - average * average
-    b_inverse = lax.rsqrt(spread + EPSILON)
+    def branch_norm():
+        pre_wait()
+        for level in range(4):
+
+            @pl.when(g == level)
+            def _():
+                span = SPANS[level]
+                for c in range(4):
+                    total = pre[c, STARTS[level]:STARTS[level] + span, :]
+                    for slot in range(3):
+                        total = total + prr[slot, c, 0:span, :]
+                    nb_s[c, 0:span, :] = total
+
+        pre_all = rows_of(nb_s[...])
+        average = jnp.sum(pre_all, 0, keepdims=True) / samples
+        spread = jnp.sum(pre_all * pre_all, 0, keepdims=True) / samples - average * average
+        b_inverse = lax.rsqrt(spread + EPSILON)
+        b_norm = (pre_all - average) * b_inverse
+        b_act = b_gain * b_norm + bbias[pl.ds(g, 1), :]
+        nb_s[...] = b_norm.reshape(4, WIDE, 128)
+        bi_s[0:1, :] = b_inverse
+        logistic = jax.nn.sigmoid(b_act)
+        af_s[...] = (logistic * (1.0 + b_act * (1.0 - logistic))).reshape(4, WIDE, 128)
+        bos[...] = (b_act * logistic).astype(bf16).reshape(4, WIDE, 128)
+        each(bo_copies, "start")()
+        bor[z] = bos[...]
+
     b_gain = bgain[pl.ds(g, 1), :]
-    b_norm = (pre_all - average) * b_inverse
-    b_act = b_gain * b_norm + bbias[pl.ds(g, 1), :]
-    nb_s[...] = b_norm.reshape(4, WIDE, 128)
-    logistic = jax.nn.sigmoid(b_act)
-    af_s[...] = (logistic * (1.0 + b_act * (1.0 - logistic))).reshape(4, WIDE, 128)
-    bos[...] = (b_act * logistic).astype(bf16).reshape(4, WIDE, 128)
-
     f_send, f_recv = names.take(3), names.take(3)
-
-    def share(ref, at):
-        return ref.at[:, pl.ds(0, WIDE), pl.ds(pl.multiple_of(128 * at, 128), 128)]
-
-    for j in (1, 2, 3):
-        copy(bos, share(bo, z), f_send + j - 1, f_recv + j - 1, zpeer(j)).start()
-    bo[:, 0:WIDE, pl.ds(pl.multiple_of(128 * z, 128), 128)] = bos[...]
-    for j in (1, 2, 3):
-        copy(bos, share(bo, lax.rem(z + 4 - j, 4)), f_send + j - 1, f_recv + j - 1, zpeer(j)).wait_recv()
+    bo_copies = [copy(bos, bor.at[z], f_send + j - 1, f_recv + j - 1, zpeer(j)) for j in (1, 2, 3)]
+    finals.append(each(bo_copies, "wait_send"))
 
     i_send, i_recv = names.take(12), names.take(12)
 
@@ -363,26 +501,95 @@
         dev, _ = peer(kx, ky, 0)
         return copy(p.at[c, :, chip_rows(dev["ha"]), :], cr.at[slot, c], i_send + 4 * slot + c, i_recv + 4 * slot + c, dev)
 
-    def level_conv(c, carry):
-        lv[c] = (dot(uh[c], bo[c]) + dot(ul[c], bo[c])).astype(bf16)
-        out0, out1 = conv_part(lv[c], 1)
-        p[c, 0] = p[c, 0] + out0
-        p[c, 1] = p[c, 1] + out1
+    def conv_send(c):
         for kx, ky in chips:
             conv_copy(c, kx, ky).start()
-        return carry
-
-    lax.fori_loop(0, 4, level_conv, 0)
-
-    for j in (1, 2, 3):
-        src = lax.rem(z + 4 - j, 4)
-        copy(sd.at[src], sd.at[src], sz_send + j - 1, sz_recv + j - 1, zpeer(j)).wait_recv()
+
+    def far(c):
+        return (c + z == 3) & ((c == 0) | (c == 3))
+
+    def levels(core):
+        each(bo_copies, "wait_recv")()
+        for part in range(4):
+            for half in range(2):
+                bo2[:, 128 * half:128 * half + WIDE, 128 * part:128 * part + 128] = bor[part]
+
+        def level_conv(c, carry):
+            lv[c] = dot(u2[c], bo2[c]).astype(bf16)
+            conv_add(c, lv[c], 1)
+            if core == 0:
+                pl.when(jnp.logical_not(far(c)))(lambda: conv_send(c))
+            else:
+                conv_send(c)
+            return carry
+
+        lax.fori_loop(0, 4, level_conv, 0)
+
+    @pl.when(w == 0)
+    def _():
+        def one(j, carry):
+            src = lax.rem(z + 4 - j, 4)
+            copy(po.at[src], po.at[src], h_send + j - 1, h_recv + j - 1, zpeer(j)).wait_recv()
+            branch_products(src)
+            return carry
+
+        lax.fori_loop(1, 4, one, 0)
+
+    @pl.when((w == 1) & (zm == 0))
+    def _():
+        own_turn(True)
+        own_turn(False)
+
+    @pl.when((w == 1) & (zm == 1))
+    def _():
+        own_turn(False)
+        own_turn(True)
+
+    def arrived(c):
+        @pl.when(w == 1)
+        def _():
+            pool(c)
+            branch_products(c)
+
+        pl.when(w == 0)(lambda: conv_add(c, x[c], 0))
+
+    for k in (1, 2, 3):
+        if k < 3:
+            give_turn(k - 1)
+        for h in range(2):
+            take_in(k, h)
+            if k < 3:
+                pass_on(k, h)
+        pl.when(z >= k)(lambda: arrived(z - k))
+        pl.when(z + k <= 3)(lambda: arrived(z + k))
+        if k == 1:
+            pl.when(w == 0)(branch_norm)
+        if k == 2:
+            pl.when(w == 0)(lambda: levels(0))
+
+    pl.when((w == 0) & far(3 - z))(lambda: conv_send(3 - z))
+
+    @pl.when(w == 1)
+    def _():
+        branch_norm()
+
+        def late(j, carry):
+            c = lax.rem(z + j, 4)
+            conv_add(c, x[c], 0)
+            return carry
+
+        lax.fori_loop(1, 4, late, 0)
+        levels(1)
+
+    conv_copies = [conv_copy(c, kx, ky) for c in range(4) for kx, ky in chips]
+    due["conv"] = each(conv_copies, "wait_recv")
+    finals.append(each(conv_copies, "wait_send"))
+
+    arrive("sd")
     for c in range(4):
         cn_s[0, 128 * c:128 * c + 128, :] = dot(sd[c], cwt[...], ROWS_T, FULL_ACCURACY)
 
-    for c in range(4):
-        for kx, ky in chips:
-            conv_copy(c, kx, ky).wait_recv()
+    arrive("conv")
     convolved = (p[:, :, pl.ds(q64, 64), :] + cr[0] + cr[1] + cr[2]).reshape(512, 128)
     ok = val.at[...].reshape(4, 2, 256, 128)[:, :, pl.ds(q64, 64), :].reshape(512, 128)
 
@@ -397,10 +604,10 @@
     def plane_sum(stage, first, second):
         st[stage, 0:1, :] = first
         st[stage, 1:2, :] = second
-        for kx, ky in chips:
-            stat_copy(stage, kx, ky).start()
-        for kx, ky in chips:
-            stat_copy(stage, kx, ky).wait_recv()
+        copies = [stat_copy(stage, kx, ky) for kx, ky in chips]
+        each(copies, "start")()
+        each(copies, "wait_recv")()
+        finals.append(each(copies, "wait_send"))
         total = st[stage] + str_[stage, 0] + str_[stage, 1] + str_[stage, 2]
         return total[0:1], total[1:2]
 
@@ -438,24 +645,12 @@
         block = gc.at[:, :, chip_rows(at), :]
         return copy(block, block, k_send + slot, k_recv + slot, peer(kx, ky, 0)[0])
 
-    for kx, ky in chips:
-        gc_copy(kx, ky, q).start()
-
-    lt_send, lt_recv = names.take(3), names.take(3)
-    weight_part = jnp.zeros((24, 128), f32)
-    bias_part = jnp.zeros((24, 1), f32)
-    for c in range(4):
-        hidden_c = cn_s[1, 128 * c:128 * c + 128, :]
-        lt[c] = dot(cwt[...], hidden_c, BOTH_LAST, FULL_ACCURACY)
-        weight_part = weight_part + dot(sd[c], hidden_c, precision=FULL_ACCURACY)
-        bias_part = bias_part + jnp.sum(sd[c], 1, keepdims=True)
-    small[0:24, :] = weight_part
-    small[24:48, :] = jnp.broadcast_to(bias_part, (24, 128))
-    for j in (1, 2, 3):
-        copy(lt.at[lax.rem(z + j, 4)], ltr.at[j - 1], lt_send + j - 1, lt_recv + j - 1, zpeer(j)).start()
-
-    for kx, ky in chips:
-        gc_copy(kx, ky, peer(kx, ky, 0)[0]["ha"]).wait_recv()
+    gc_copies = [gc_copy(kx, ky, q) for kx, ky in chips]
+    each(gc_copies, "start")()
+    due["gc"] = each(gc_copies, "wait_recv")
+    finals.append(each(gc_copies, "wait_send"))
+
+    arrive("gc")
 
     def shifted(c):
         col = lax.broadcasted_iota(jnp.int32, (256, 128), 0) % 8
@@ -474,14 +669,17 @@
                     start = 8 * (2 - a)
                     g9[c, 256 * h:256 * h + 256, 128 * t:128 * t + 128] = gp3[b, h, start:start + 256, :].astype(bf16)
 
+    def level_rows(c, carry):
+        shifted(c)
+        both = dot(ut[c], g9[c])
+        high, low = halves(both[0:128] + both[128:256])
+        tb[c, 0:128, :] = high
+        tb[c, 128:256, :] = low
+        return carry
+
     def data_grad(c):
-        shifted(c)
         for h in range(2):
             dxf[c, 256 * h:256 * h + 256, :] = dot(g9[c, 256 * h:256 * h + 256, :], wall[0:512, :], BOTH_LAST)
-        back = dot(g9[c], wall[512:1024, :], BOTH_LAST)
-        high, low = halves(back)
-        total = dot(uh[c], high, ROWS_T) + dot(uh[c], low, ROWS_T) + dot(ul[c], high, ROWS_T)
-        gb[c] = total[0:WIDE].astype(bf16)
 
     ru_send, ru_recv, rd_send, rd_recv = names.take(3), names.take(3), names.take(3), names.take(3)
 
@@ -497,60 +695,71 @@
     def dn_on(k):
         return (z - 3 + k >= 0) & (z > 0)
 
-    def scatter_step(k):
-        @pl.when(up_on(k))
+    def end_send(k):
+        @pl.when(z == 0)
         def _():
-            value = dxf[z + 3 - k]
-            if k:
-                sbu[k] = value.astype(bf16)
-
-                @pl.when(z > 0)
-                def _():
-                    ru_copy(k - 1).wait_recv()
-                    sbu[k] = (value + rxu[k - 1].astype(f32)).astype(bf16)
-            else:
-                sbu[k] = value.astype(bf16)
+            sbu[k] = dxf[3 - k].astype(bf16)
             ru_copy(k).start()
 
-        @pl.when(dn_on(k))
+        @pl.when(z == 3)
         def _():
-            value = dxf[z - 3 + k]
-            if k:
-                sbd[k] = value.astype(bf16)
-
-                @pl.when(z < 3)
-                def _():
-                    rd_copy(k - 1).wait_recv()
-                    sbd[k] = (value + rxd[k - 1].astype(f32)).astype(bf16)
-            else:
-                sbd[k] = value.astype(bf16)
+            sbd[k] = dxf[k].astype(bf16)
             rd_copy(k).start()
+
+    def middle_send(k):
+        @pl.when(up_on(k) & (z > 0))
+        def _():
+            ru_copy(k - 1).wait_recv()
+            sbu[k] = (dxf[z + 3 - k] + rxu[k - 1].astype(f32)).astype(bf16)
+            ru_copy(k).start()
+
+        @pl.when(dn_on(k) & (z < 3))
+        def _():
+            rd_copy(k - 1).wait_recv()
+            sbd[k] = (dxf[z - 3 + k] + rxd[k - 1].astype(f32)).astype(bf16)
+            rd_copy(k).start()
+
+    def scatter_sent():
+        for k in range(3):
+            pl.when(up_on(k))(lambda: ru_copy(k).wait_send())
+            pl.when(dn_on(k))(lambda: rd_copy(k).wait_send())
 
     def canvas_at(i):
         low = (3 - i) if i < 2 else zz * (i - 2) + (1 - zz) * (3 - i)
         return (1 - zm) * low + zm * (3 - low)
 
-    for i in range(4):
-        data_grad(canvas_at(i))
-        if i == 0:
-            scatter_step(0)
-
     n_send, n_recv = names.take(3), names.take(3)
-    for level in range(4):
-
-        @pl.when(g == level)
-        def _():
-            for j in (1, 2, 3):
-                at = lax.rem(z + j, 4)
-                copy(
-                    gb.at[:, pl.ds(0, SPANS[level]), pl.ds(pl.multiple_of(128 * at, 128), 128)],
-                    grr.at[j - 1, :, pl.ds(0, SPANS[level]), :],
-                    n_send + j - 1, n_recv + j - 1, zpeer(j),
-                ).start()
-
-    scatter_step(1)
-
-    def weight_grad(part, store):
+
+    def gb_copies(method):
+        for level in range(4):
+
+            @pl.when(g == level)
+            def _():
+                for j in (1, 2, 3):
+                    item = copy(
+                        gb.at[lax.rem(z + j, 4), :, pl.ds(0, SPANS[level]), :],
+                        grr.at[j - 1, :, pl.ds(0, SPANS[level]), :],
+                        n_send + j - 1, n_recv + j - 1, zpeer(j),
+                    )
+                    getattr(item, method)()
+
+    lax.fori_loop(0, 4, level_rows, 0)
+
+    def level_pair(n, carry):
+        both = dot(tb[pl.ds(2 * n, 2)].reshape(512, 1152), wall[512:1024, :], BOTH_LAST)
+        for c in range(2):
+            total = both[256 * c:256 * c + WIDE] + both[256 * c + 128:256 * c + 128 + WIDE]
+            for part in range(4):
+                gb[part, 2 * n + c] = total[:, 128 * part:128 * part + 128].astype(bf16)
+        return carry
+
+    lax.fori_loop(0, 2, level_pair, 0)
+    gb_copies("start")
+    due["gb"] = lambda: gb_copies("wait_recv")
+    finals.append(lambda: gb_copies("wait_send"))
+
+    def weight_grad(part, slot):
+
         for tile in range(2):
             cols = slice(256 * tile, 256 * tile + 256)
 
@@ -559,96 +768,77 @@
                 for c in range(4):
                     piece = dot(operand[c, :, cols], g9[c], ROWS_T)
                     total = piece if total is None else total + piece
-                store(tile, total)
+                dw[slot, cols, :] = total
 
             pl.when(part == 0)(lambda: of(x))
             pl.when(part == 1)(lambda: of(lv))
 
-    def store_out(tile, total):
-        dw[0, 256 * tile:256 * tile + 256, :] = total
-
-    def store_own(tile, total):
-        dw[1, 256 * tile:256 * tile + 256, :] = total
-
-    weight_grad(1 - w, store_out)
     w_send, w_recv = names.take(), names.take()
-    dw_copy = copy(dw.at[0], dwr, w_send, w_recv, peer(0, 0, 1)[0])
-    dw_copy.start()
-    weight_grad(w, store_own)
-
+    dw_copy = copy(dw.at[0], dwr, w_send, w_recv, other)
+    y_send, y_recv = names.take(), names.take()
+    dw_y = copy(dwh, dwx, y_send, y_recv, {"ha": peer(0, 1, 0)[0]["ha"], "wa": yq})
+    b_send, b_recv = names.take(), names.take()
+    dw_back = copy(dw.at[1], dwr, b_send, b_recv, other)
+    cg_sem = names.take()
+
+    def cg_out(src):
+        return pltpu.make_async_copy(src, cgrad_out, sems.at[cg_sem])
+
+    weight_grad(1 - yq, w)
+    pl.when(w == 0)(lambda: dw_copy.start())
+
+    @pl.when(w == 1)
+    def _():
+        dw_copy.wait_recv()
+        dwh[...] = (dw[1] + dwr[...]).astype(bf16)
+        dw_y.start()
+
+    for i in range(4):
+        data_grad(canvas_at(i))
+        if i < 3:
+            end_send(i)
+
+    arrive("gb")
     for level in range(4):
 
         @pl.when(g == level)
         def _():
-            for j in (1, 2, 3):
-                copy(
-                    gb.at[:, pl.ds(0, SPANS[level]), pl.ds(0, 128)],
-                    grr.at[j - 1, :, pl.ds(0, SPANS[level]), :],
-                    n_send + j - 1, n_recv + j - 1, zpeer(j),
-                ).wait_recv()
-
-    own_grad = gb[:, :, pl.ds(pl.multiple_of(128 * z, 128), 128)].astype(f32)
-    for j in range(3):
-        own_grad = own_grad + grr[j].astype(f32)
-    grad_act = rows_of(own_grad) * rows_of(af_s[...])
+            span = SPANS[level]
+            total = gb[z, :, 0:span, :].astype(f32)
+            for j in range(3):
+                total = total + grr[j, :, 0:span, :].astype(f32)
+            gpre[:, 0:span, :] = total
+
+    grad_act = rows_of(gpre[...]) * rows_of(af_s[...])
     b_norm = rows_of(nb_s[...])
     act_sum = jnp.sum(grad_act, 0, keepdims=True)
     act_norm_sum = jnp.sum(grad_act * b_norm, 0, keepdims=True)
     small[50:51, :] = act_norm_sum
     small[51:52, :] = act_sum
-    grad_pre = b_inverse * (
+    grad_pre = bi_s[0:1, :] * (
         b_gain * grad_act - b_gain * act_sum / samples - b_norm * b_gain * act_norm_sum / samples
     )
     gpre[...] = grad_pre.reshape(4, WIDE, 128)
     o_send, o_recv = names.take(3), names.take(12)
-    for level in range(4):
-
-        @pl.when(g == level)
-        def _():
-            rows = pl.ds(STARTS[level], SPANS[level])
-            for kx, ky in chips:
-                slot = kx + 2 * ky - 1
-                copy(
-                    gpre.at[:, pl.ds(0, SPANS[level]), :], gpa.at[:, rows, :],
-                    o_send + slot, o_recv + 3 * level + slot, peer(kx, ky, 0)[0],
-                ).start()
-            gpa[:, STARTS[level]:STARTS[level] + SPANS[level], :] = gpre[:, 0:SPANS[level], :]
-
-    s_send, s_recv = names.take(7), names.take(7)
-
-    def small_copy(n):
-        return copy(small, smr.at[n], s_send + n, s_recv + n, peer(*plane[n])[0])
-
-    for n in range(7):
-        small_copy(n).start()
-
-    dw_copy.wait_recv()
-    dw[1] = dw[1] + dwr[...]
-    y_send, y_recv = names.take(9), names.take(9)
-    y_dev = peer(0, 1, 1)[0]
-
-    def tap_copy(t):
-        return copy(dw.at[1, :, pl.ds(128 * t, 128)], cgrad_out.at[t], y_send + t, y_recv + t, y_dev)
-
-    def tap_own(t):
-        return pltpu.make_async_copy(dw.at[1, :, pl.ds(128 * t, 128)], cgrad_out.at[t], sems.at[y_send + t])
-
-    @pl.when(w == yq)
-    def _():
-        for t in range(TAPS):
-            tap_own(t).start()
-
-    @pl.when(w != yq)
-    def _():
-        for t in range(TAPS):
-            tap_copy(t).start()
-
-    for level in range(4):
-        lx, ly = level // 2, level % 2
-        for kx, ky in chips:
-
-            @pl.when((xq + kx - 2 * kx * xq == lx) & (yq + ky - 2 * ky * yq == ly))
+
+    def gpre_copies(method):
+        for level in range(4):
+
+            @pl.when(g == level)
             def _():
+                rows = pl.ds(STARTS[level], SPANS[level])
+                for kx, ky in chips:
+                    slot = kx + 2 * ky - 1
+                    c = copy(
+                        gpre.at[:, pl.ds(0, SPANS[level]), :], gpa.at[:, rows, :],
+                        o_send + slot, o_recv + 3 * level + slot, peer(kx, ky, 0)[0],
+                    )
+                    getattr(c, method)()
+
+    def gpre_wait():
+        for level in range(4):
+
+            def wait(kx, ky):
                 slot = kx + 2 * ky - 1
                 copy(
                     gpre.at[:, pl.ds(0, SPANS[level]), :],
@@ -656,35 +846,78 @@
                     o_send + slot, o_recv + 3 * level + slot, peer(kx, ky, 0)[0],
                 ).wait_recv()
 
-    def pooled_grad(c, carry):
-        for level in range(4):
-            rows = slice(STARTS[level], STARTS[level] + SPANS[level])
-            high, low = halves(gpa[c, rows, :])
-            gps[c, rows, :] = (dot(high, wb[level], BOTH_LAST) + dot(low, wb[level], BOTH_LAST)).astype(bf16)
+            to_level_owner(level, wait)
+
+    gpre_copies("start")
+    for level in range(4):
+
+        @pl.when(g == level)
+        def _():
+            gpa[:, STARTS[level]:STARTS[level] + SPANS[level], :] = gpre[:, 0:SPANS[level], :]
+
+    due["gpre"] = gpre_wait
+    finals.append(lambda: gpre_copies("wait_send"))
+
+    middle_send(1)
+
+    lt_send, lt_recv = names.take(3), names.take(3)
+    weight_part = jnp.zeros((24, 128), f32)
+    bias_part = jnp.zeros((24, 1), f32)
+    for c in range(4):
+        hidden_c = cn_s[1, 128 * c:128 * c + 128, :]
+        lt[c] = dot(cwt[...], hidden_c, BOTH_LAST, FULL_ACCURACY)
+        weight_part = weight_part + dot(sd[c], hidden_c, precision=FULL_ACCURACY)
+        bias_part = bias_part + jnp.sum(sd[c], 1, keepdims=True)
+    small[0:24, :] = weight_part
+    small[24:48, :] = jnp.broadcast_to(bias_part, (24, 128))
+    lt_copies = [
+        copy(lt.at[lax.rem(z + j, 4)], ltr.at[j - 1], lt_send + j - 1, lt_recv + j - 1, zpeer(j)) for j in (1, 2, 3)
+    ]
+    each(lt_copies, "start")()
+    due["lt"] = each(lt_copies, "wait_recv")
+    finals.append(each(lt_copies, "wait_send"))
+
+    arrive("gpre")
+
+    def split_rows(c, carry):
+        high, low = halves(gpa[c])
+        gpx[c, :, 0:128] = high
+        gpx[c, :, 128:256] = low
         return carry
 
-    lax.fori_loop(0, 4, pooled_grad, 0)
-    p_send, p_recv = names.take(3), names.take(3)
-    for j in (1, 2, 3):
-        copy(gps.at[lax.rem(z + j, 4)], gpr.at[j - 1], p_send + j - 1, p_recv + j - 1, zpeer(j)).start()
-
-    scatter_step(2)
+    lax.fori_loop(0, 4, split_rows, 0)
 
     for level in range(4):
         rows = slice(STARTS[level], STARTS[level] + SPANS[level])
         total = None
         for c in range(4):
-            high, low = halves(gpa[c, rows, :])
-            piece = dot(po[c, rows, :], high, ROWS_T) + dot(po[c, rows, :], low, ROWS_T)
+            piece = dot(po[c, rows, :], gpx[c, rows, :], ROWS_T)
             total = piece if total is None else total + piece
-        bg[level] = total
+        bg[level] = total[:, 0:128] + total[:, 128:256]
     bc_send, bc_recv = names.take(), names.take()
     w256 = pl.multiple_of(256 * w, 256)
     v256 = pl.multiple_of(256 * (1 - w), 256)
     bg_copy = copy(bg.at[:, pl.ds(v256, 256), :], bgr, bc_send, bc_recv, peer(0, 0, 1)[0])
     bg_copy.start()
-    bg_copy.wait_recv()
-    bgh[...] = (bg[:, pl.ds(w256, 256), :] + bgr[...]).astype(bf16)
+    due["bgc"] = bg_copy.wait_recv
+    finals.append(bg_copy.wait_send)
+
+    def pooled_grad(c, carry):
+        for level in range(4):
+            rows = slice(STARTS[level], STARTS[level] + SPANS[level])
+            gps[c, rows, :] = dot(gpx[c, rows, :], wb2[level], BOTH_LAST).astype(bf16)
+        return carry
+
+    lax.fori_loop(0, 4, pooled_grad, 0)
+    p_send, p_recv = names.take(3), names.take(3)
+    gp_copies = [
+        copy(gps.at[lax.rem(z + j, 4)], gpr.at[j - 1], p_send + j - 1, p_recv + j - 1, zpeer(j)) for j in (1, 2, 3)
+    ]
+    each(gp_copies, "start")()
+    due["gp"] = each(gp_copies, "wait_recv")
+    finals.append(each(gp_copies, "wait_send"))
+
+    bg_wait = due.pop("bgc")
     own_channels = pl.ds(pl.multiple_of(512 * g + 256 * w, 256), 256)
     bx_send, bx_recv = names.take(3), names.take(3)
     by_send, by_recv = names.take(4), names.take(4)
@@ -699,63 +932,153 @@
     def bg_core(n, block):
         return copy(bga_of(block, w), bga_of(block, w), by_send + n, by_recv + n, peer(0, 0, 1)[0])
 
-    for kx, ky in chips:
-        bg_chip(kx, ky).start()
-    bga[:, own_channels, :] = bgh[...]
-    bg_core(3, g).start()
-
-    for j in (1, 2, 3):
-        copy(lt.at[0], ltr.at[j - 1], lt_send + j - 1, lt_recv + j - 1, zpeer(j)).wait_recv()
+    bg_copies = [bg_chip(kx, ky) for kx, ky in chips]
+    due["bg"] = each(bg_copies, "wait_recv")
+    finals.append(each(bg_copies, "wait_send"))
+    bg_own = bg_core(3, g)
+    finals.append(bg_own.wait_send)
+    due["by", 3] = bg_own.wait_recv
+
+    def bg_sum():
+        bg_wait()
+        bgh[...] = (bg[:, pl.ds(w256, 256), :] + bgr[...]).astype(bf16)
+        each(bg_copies, "start")()
+        bga[:, own_channels, :] = bgh[...]
+        bg_own.start()
+
+    pl.when(w == 1)(bg_sum)
+
+    middle_send(2)
+    finals.append(scatter_sent)
+
+    weight_grad(yq, 1 - w)
+    pl.when(w == 1)(lambda: dw_copy.start())
+
+    def dw_sum():
+        @pl.when(w == 0)
+        def _():
+            dw_copy.wait_recv()
+            dw[1] = dw[1] + dwr[...]
+            pl.when(yq == 0)(lambda: cg_out(dw.at[1]).start())
+            pl.when(yq == 1)(lambda: dw_back.start())
+
+    def dw_place():
+        @pl.when((w == 1) & (yq == 1))
+        def _():
+            dw_back.wait_recv()
+            cg_out(dwr).start()
+
+        dw_copy.wait_send()
+
+        @pl.when(w != yq)
+        def _():
+            dw_y.wait_recv()
+            dw[0] = dwx[...].astype(f32)
+            cg_out(dw.at[0]).start()
+
+    due["dw"] = dw_sum
+    due["dwy"] = dw_place
+    finals.append(lambda: cg_out(dw.at[0]).wait())
+    finals.append(lambda: pl.when(w == 1)(lambda: dw_y.wait_send()))
+    finals.append(lambda: pl.when((w == 0) & (yq == 1))(lambda: dw_back.wait_send()))
+
+    s_send, s_recv = names.take(7), names.take(7)
+
+    def small_copy(n):
+        return copy(small, smr.at[n], s_send + n, s_recv + n, peer(*plane[n])[0])
+
+    small_copies = [small_copy(n) for n in range(7)]
+    each(small_copies, "start")()
+    due["small"] = each(small_copies, "wait_recv")
+    finals.append(each(small_copies, "wait_send"))
+
+
+    gp_wait = due.pop("gp")
+
+    def ru_wait():
+        pl.when(z > 0)(lambda: ru_copy(2).wait_recv())
+
+    def rd_wait():
+        pl.when(z < 3)(lambda: rd_copy(2).wait_recv())
+
+    q_send, q_recv = names.take(8), names.take(8)
+
+    def fg_copy(n):
+        dev, _ = peer(*plane[n])
+        rows = pl.ds(pl.multiple_of(256 * dev["wa"] + 64 * dev["ha"], 64), 64)
+        return copy(fgh.at[rows, :], fgrad_out.at[w, :, pl.ds(g512, 512)], q_send + n, q_recv + n, dev)
+
+    fg_copies = [fg_copy(n) for n in range(7)]
+    finals.append(each(fg_copies, "wait_send"))
+    fg_own = pltpu.make_async_copy(
+        fgh.at[pl.ds(own_row, 64), :], fgrad_out.at[w, :, pl.ds(g512, 512)], sems.at[q_send + 7]
+    )
+    finals.append(fg_own.wait)
+
+    def fg_wait():
+        for n in range(7):
+            dev, block = peer(*plane[n])
+            copy(
+                fgh.at[pl.ds(0, 64), :],
+                fgrad_out.at[dev["wa"], :, pl.ds(pl.multiple_of(512 * block, 512), 512)],
+                q_send + n, q_recv + n, dev,
+            ).wait_recv()
+
+    finals.append(fg_wait)
+
+    def feature_grads():
+        gp_wait()
+        pooled_back = gps[z].astype(f32)
+        for j in range(3):
+            pooled_back = pooled_back + gpr[j].astype(f32)
+        count = cnt[z]
+        pieces = [pooled_back[:, 128 * chunk:128 * chunk + 128] / count for chunk in range(4)]
+        high, low = halves(jnp.concatenate(pieces, 1))
+        fg[...] = dot(mt[z], high, ROWS_T) + dot(mt[z], low, ROWS_T)
+        ok = val[z]
+
+        ru_wait()
+        rd_wait()
+
+        @pl.when(z > 0)
+        def _():
+            dxf[z] = dxf[z] + rxu[2].astype(f32)
+
+        @pl.when(z < 3)
+        def _():
+            dxf[z] = dxf[z] + rxd[2].astype(f32)
+
+        for chunk in range(4):
+            cols = slice(128 * chunk, 128 * chunk + 128)
+            fgh[:, cols] = (fg[:, cols] + dxf[z, :, cols] * ok).astype(bf16)
+        each(fg_copies, "start")()
+        fg_own.start()
+
+    @pl.when(w == 0)
+    def _():
+        feature_grads()
+        bg_sum()
+
+    arrive("dw")
+
+    arrive("lt")
     lts[w] = lt[z] + ltr[0] + ltr[1] + ltr[2]
     ls_send, ls_recv = names.take(), names.take()
     logits_copy = copy(lts.at[w], lts.at[w], ls_send, ls_recv, peer(0, 0, 1)[0])
     logits_copy.start()
-
-    for j in (1, 2, 3):
-        copy(gps.at[0], gpr.at[j - 1], p_send + j - 1, p_recv + j - 1, zpeer(j)).wait_recv()
-    pooled_back = gps[z].astype(f32)
-    for j in range(3):
-        pooled_back = pooled_back + gpr[j].astype(f32)
-    count = cnt[z]
-    pieces = [pooled_back[:, 128 * chunk:128 * chunk + 128] / count for chunk in range(4)]
-    high, low = halves(jnp.concatenate(pieces, 1))
-    fg[...] = dot(mt[z], high, ROWS_T) + dot(mt[z], low, ROWS_T)
-    ok = val[z]
-
-    @pl.when(z > 0)
-    def _():
-        ru_copy(2).wait_recv()
-        dxf[z] = dxf[z] + rxu[2].astype(f32)
-
-    @pl.when(z < 3)
-    def _():
-        rd_copy(2).wait_recv()
-        dxf[z] = dxf[z] + rxd[2].astype(f32)
-
-    for chunk in range(4):
-        cols = slice(128 * chunk, 128 * chunk + 128)
-        fg[:, cols] = fg[:, cols] + dxf[z, :, cols] * ok
-    q_send, q_recv = names.take(8), names.take(8)
-
-    def fg_copy(n):
-        dev, _ = peer(*plane[n])
-        rows = pl.ds(pl.multiple_of(256 * dev["wa"] + 64 * dev["ha"], 64), 64)
-        return copy(fg.at[rows, :], fgrad_out.at[w, :, pl.ds(g512, 512)], q_send + n, q_recv + n, dev)
-
-    for n in range(7):
-        fg_copy(n).start()
-    fg_own = pltpu.make_async_copy(
-        fg.at[pl.ds(own_row, 64), :], fgrad_out.at[w, :, pl.ds(g512, 512)], sems.at[q_send + 7]
-    )
-    fg_own.start()
-
+    due["ls"] = logits_copy.wait_recv
+    finals.append(logits_copy.wait_send)
+
+    pl.when(w == 1)(feature_grads)
+
+    arrive("bg")
     for n, (kx, ky) in enumerate(chips):
-        dev, block = peer(kx, ky, 0)
-        copy(bgh, bga_of(block, w), bx_send + n, bx_recv + n, dev).wait_recv()
-        bg_core(n, block).start()
-
-    for n in range(7):
-        small_copy(n).wait_recv()
+        item = bg_core(n, peer(kx, ky, 0)[1])
+        item.start()
+        finals.append(item.wait_send)
+        due["by", n] = item.wait_recv
+
+    arrive("small")
     total = small[...]
     for n in range(7):
         total = total + smr[n]
@@ -768,87 +1091,76 @@
         small_out[pl.ds(56 + block, 1), :] = both[50:51]
         small_out[pl.ds(60 + block, 1), :] = both[51:52]
 
-    logits_other = copy(lts.at[1 - w], lts.at[1 - w], ls_send, ls_recv, peer(0, 0, 1)[0])
-    logits_other.wait_recv()
-    logits_out[...] = lts[...]
-
-    for n, (kx, ky) in enumerate([*chips, (0, 0)]):
-        block = peer(kx, ky, 0)[1]
-        copy(bga_of(block, 1 - w), bga_of(block, 1 - w), by_send + n, by_recv + n, peer(0, 0, 1)[0]).wait_recv()
+    arrive("ls")
+    for micro in range(2):
+        square[:, 0:24] = lts[micro].T
+        tile = square[pl.ds(w64, 64), 0:classes] + cb[...]
+        logits_out[micro] = tile * tile_valid(micro)[:, 0:classes]
+
+    for n in range(4):
+        arrive(("by", n))
     out_sem = names.take()
     bg_out = pltpu.make_async_copy(bga, bgrad_out, sems.at[out_sem])
     bg_out.start()
 
-    for n in range(7):
-        dev, block = peer(*plane[n])
-        copy(
-            fg.at[pl.ds(0, 64), :],
-            fgrad_out.at[dev["wa"], :, pl.ds(pl.multiple_of(512 * block, 512), 512)],
-            q_send + n, q_recv + n, dev,
-        ).wait_recv()
-    fg_own.wait()
-
-    @pl.when(w == yq)
-    def _():
-        for t in range(TAPS):
-            tap_own(t).wait()
-
-    @pl.when(w != yq)
-    def _():
-        for t in range(TAPS):
-            tap_copy(t).wait()
-
-    for c in a_copies:
-        c.wait_send()
-    seed_copy.wait_send()
-    for k in range(3):
-        pl.when((z >= k) & (z < 3))(lambda: up_copy(k).wait_send())
-        pl.when((z + k <= 3) & (z > 0))(lambda: dn_copy(k).wait_send())
-        pl.when(up_on(k))(lambda: ru_copy(k).wait_send())
-        pl.when(dn_on(k))(lambda: rd_copy(k).wait_send())
-    for j in (1, 2, 3):
-        copy(sd.at[z], sd.at[z], sz_send + j - 1, sz_recv + j - 1, zpeer(j)).wait_send()
-        copy(bos, share(bo, z), f_send + j - 1, f_recv + j - 1, zpeer(j)).wait_send()
-        copy(lt.at[0], ltr.at[j - 1], lt_send + j - 1, lt_recv + j - 1, zpeer(j)).wait_send()
-        copy(gps.at[0], gpr.at[j - 1], p_send + j - 1, p_recv + j - 1, zpeer(j)).wait_send()
-    for level in range(4):
-        for c in range(4):
-            to_level_owner(level, lambda kx, ky: pre_copy(level, c, kx, ky).wait_send())
-
-        @pl.when(g == level)
-        def _():
-            for j in (1, 2, 3):
-                copy(
-                    gb.at[:, pl.ds(0, SPANS[level]), pl.ds(0, 128)],
-                    grr.at[j - 1, :, pl.ds(0, SPANS[level]), :],
-                    n_send + j - 1, n_recv + j - 1, zpeer(j),
-                ).wait_send()
-            for kx, ky in chips:
-                slot = kx + 2 * ky - 1
-                copy(
-                    gpre.at[:, pl.ds(0, SPANS[level]), :], gpa.at[:, pl.ds(STARTS[level], SPANS[level]), :],
-                    o_send + slot, o_recv + 3 * level + slot, peer(kx, ky, 0)[0],
-                ).wait_send()
-    for kx, ky in chips:
-        for c in range(4):
-            conv_copy(c, kx, ky).wait_send()
-        for stage in range(2):
-            stat_copy(stage, kx, ky).wait_send()
-        gc_copy(kx, ky, q).wait_send()
-        bg_chip(kx, ky).wait_send()
-    dw_copy.wait_send()
-    bg_copy.wait_send()
-    logits_copy.wait_send()
-    for n in range(7):
-        small_copy(n).wait_send()
-        fg_copy(n).wait_send()
-    for n in range(4):
-        bg_core(n, g).wait_send()
-    bg_out.wait()
+    finals.append(bg_out.wait)
+
+    arrive("dwy")
+
+    for wait in finals:
+        wait()
+    assert not due
     assert names.count <= SEMAPHORES
 
 
 SEMAPHORES = 256
+
+
+def place_kernel(
+    logits, fgrad, bgrad, small, cgrad,
+    logits_out, fgrad_out, bgrad_out, gains_out, biases_out, cgrad_out, gain_out, bias_out, weight_out, class_out,
+    low, wide, feats, feats_wide, taps, square, sems,
+):
+    levels, classes, micros = bgrad.shape[0], class_out.shape[1], fgrad.shape[0]
+    half = bgrad.shape[1] // 2
+    pieces = [(n, pl.ds(half * h, half)) for n in range(levels) for h in range(2)]
+    count = len(pieces)
+    loads = [pltpu.make_async_copy(bgrad.at[p], low.at[p], sems.at[n]) for n, p in enumerate(pieces)]
+    loads += [pltpu.make_async_copy(fgrad.at[m], feats.at[m], sems.at[count + m]) for m in range(micros)]
+    tap_load = pltpu.make_async_copy(cgrad, taps, sems.at[count + micros])
+    for load in loads:
+        load.start()
+    tap_load.start()
+    first = count + micros + 1
+    stores = [pltpu.make_async_copy(wide.at[p], bgrad_out.at[p], sems.at[first + n]) for n, p in enumerate(pieces)]
+    stores += [
+        pltpu.make_async_copy(feats_wide.at[m], fgrad_out.at[m], sems.at[first + count + m]) for m in range(micros)
+    ]
+    tap_stores = [
+        pltpu.make_async_copy(taps.at[:, pl.ds(128 * t, 128)], cgrad_out.at[t], sems.at[first + count + micros + t])
+        for t in range(TAPS)
+    ]
+    for n, p in enumerate(pieces):
+        loads[n].wait()
+        wide[p] = low[p].astype(jnp.float32)
+        stores[n].start()
+    for m in range(micros):
+        loads[count + m].wait()
+        feats_wide[m] = feats[m].astype(jnp.float32)
+        stores[count + m].start()
+    tap_load.wait()
+    for store in tap_stores:
+        store.start()
+    logits_out[...] = logits[...]
+    gains_out[...] = small[56:60, :]
+    biases_out[...] = small[60:64, :]
+    gain_out[...] = small[49:50, :]
+    bias_out[...] = small[48:49, :]
+    weight_out[...] = small[0:classes, :]
+    square[...] = small[...]
+    class_out[...] = square[24:56, :].T[0:1, 0:classes]
+    for store in stores + tap_stores:
+        store.wait()
 
 
 def canvas_body(
@@ -859,18 +1171,6 @@
     micros, tile_rows, tile_cols, channels = features.shape
     pixels = tile_rows * tile_cols
     classes = class_bias.shape[0]
-    z, w = lax.axis_index("col"), lax.axis_index("wa")
-    own_boxes = lax.dynamic_slice_in_dim(region_boxes, micros * z, micros, 0)
-    at = jnp.arange(pixels, dtype=jnp.int32)
-    y = (lax.axis_index("ha") * tile_rows + at // tile_cols)[None, None]
-    xx = (w * tile_cols + at % tile_cols)[None, None]
-    top, left, bottom, right = [own_boxes[:, :, e, None] for e in range(4)]
-    valid = jnp.any((y >= top) & (y < bottom) & (xx >= left) & (xx < right), 1).astype(f32)
-    seeds = jnp.transpose((cotangent.reshape(micros, pixels, classes) * valid[:, :, None]), (0, 2, 1))
-    seeds = jnp.pad(seeds, ((0, 0), (0, 24 - classes), (0, 0)))
-    blank = jnp.zeros_like(seeds)
-    seeds = jnp.where(w == 0, jnp.concatenate([seeds, blank], 2), jnp.concatenate([blank, seeds], 2))
-    cwt = jnp.pad(class_weight.T, ((0, 24 - classes), (0, 0)))
     lane_table, row_table = bin_tables()
 
     vmem = pl.BlockSpec(memory_space=pltpu.VMEM)
@@ -881,16 +1181,17 @@
         V((4, 512, 512), bf16),
         V((4, 512, 512), bf16),
         V((1024, 1152), bf16),
-        V((4, 512, 128), bf16),
-        V((4, 512, 128), bf16),
-        V((4, 512, 128), bf16),
+        V((4, 512, 256), bf16),
+        V((4, 512, 256), bf16),
+        V((4, 256, 512), bf16),
         V((4, BINS, 512), bf16),
         V((4, BINS, 128), f32),
         V((4, BINS, 512), bf16),
         V((4, BINS, 128), f32),
         V((3, 4, WIDE, 128), f32),
         V((4, WIDE, 128), bf16),
-        V((4, 128, 512), bf16),
+        V((4, 4, WIDE, 128), bf16),
+        V((4, 256, 512), bf16),
         V((4, 512, 128), f32),
         V((2, 272, 1152), f32),
         V((4, 2, 256, 128), f32),
@@ -898,15 +1199,17 @@
         V((4, 2, 256, 128), bf16),
         V((4, 512, 1152), bf16),
         V((3, 2, 272, 128), f32),
+        V((4, 256, 1152), bf16),
         V((4, 512, 512), f32),
         V((3, 512, 512), bf16),
         V((3, 512, 512), bf16),
         V((3, 512, 512), bf16),
         V((3, 512, 512), bf16),
-        V((4, WIDE, 512), bf16),
+        V((4, 4, WIDE, 128), bf16),
         V((3, 4, WIDE, 128), bf16),
         V((4, WIDE, 128), f32),
         V((4, BINS, 128), f32),
+        V((4, BINS, 256), bf16),
         V((4, BINS, 512), bf16),
         V((3, BINS, 512), bf16),
         V((2, 512, 1152), f32),
@@ -928,41 +1231,71 @@
         V((2, 512, 128), f32),
         V((4, channels, 128), bf16),
         V((512, 512), f32),
+        V((512, 512), bf16),
+        V((24, 128), f32),
+        V((2, 24, 128), f32),
+        V((128, 128), f32),
+        V((512, 1152), bf16),
+        V((512, 1152), bf16),
+        V((8, 128), f32),
         pltpu.SemaphoreType.DMA((SEMAPHORES,)),
+        pltpu.SemaphoreType.REGULAR((2,)),
     ]
     share = conv_weight.shape[2]
-    logits_t, feature_grad, branch_grad, small, conv_grad = pl.pallas_call(
+    parts = pl.pallas_call(
         head_kernel,
         out_shape=(
-            jax.ShapeDtypeStruct((2, 24, 128), f32),
-            jax.ShapeDtypeStruct((micros, pixels, channels), f32),
+            jax.ShapeDtypeStruct((micros, pixels, classes), f32),
+            jax.ShapeDtypeStruct((micros, pixels, channels), bf16),
             jax.ShapeDtypeStruct((4, channels, share), bf16),
             jax.ShapeDtypeStruct((64, 128), f32),
-            jax.ShapeDtypeStruct((TAPS, 512, share), f32),
+            jax.ShapeDtypeStruct((512, TAPS * share), f32),
         ),
-        in_specs=[smem, vmem, vmem, hbm, vmem, hbm, hbm, vmem, vmem, vmem, vmem, vmem],
+        in_specs=[smem, vmem, vmem, hbm, vmem, hbm, hbm, vmem, vmem, vmem, vmem, vmem, vmem],
         out_specs=(vmem, hbm, hbm, vmem, hbm),
         scratch_shapes=scratch,
         compiler_params=pltpu.CompilerParams(
             collective_id=0, has_side_effects=True, vmem_limit_bytes=60 * 2**20
         ),
     )(
-        region_boxes.reshape(-1), lane_table, row_table, features.reshape(micros, pixels, channels), seeds,
-        conv_weight, branch_weight, branch_gain, branch_bias, norm_gain.reshape(1, -1), norm_bias.reshape(1, -1), cwt,
+        jnp.transpose(region_boxes, (1, 2, 0)), lane_table, row_table, features.reshape(micros, pixels, channels),
+        cotangent.reshape(micros, pixels, classes), conv_weight, branch_weight, branch_gain, branch_bias,
+        norm_gain.reshape(1, -1), norm_bias.reshape(1, -1), class_weight.T, class_bias.reshape(1, -1),
     )
-    tile = lax.dynamic_slice_in_dim(logits_t, w * pixels, pixels, 2)[:, :classes]
-    logits = (jnp.transpose(tile, (0, 2, 1)) + class_bias) * valid[:, :, None]
+    logits, feature_grad, branch_grad, gains, biases, conv_grad, gain, bias, weight, class_grad = pl.pallas_call(
+        place_kernel,
+        out_shape=(
+            jax.ShapeDtypeStruct((micros, pixels, classes), f32),
+            jax.ShapeDtypeStruct((micros, pixels, channels), f32),
+            jax.ShapeDtypeStruct((4, channels, share), f32),
+            jax.ShapeDtypeStruct((4, share), f32),
+            jax.ShapeDtypeStruct((4, share), f32),
+            jax.ShapeDtypeStruct((TAPS, 512, share), f32),
+            jax.ShapeDtypeStruct((1, share), f32),
+            jax.ShapeDtypeStruct((1, share), f32),
+            jax.ShapeDtypeStruct((classes, share), f32),
+            jax.ShapeDtypeStruct((1, classes), f32),
+        ),
+        in_specs=[vmem, hbm, hbm, vmem, hbm],
+        out_specs=(vmem, hbm, hbm, vmem, vmem, hbm, vmem, vmem, vmem, vmem),
+        scratch_shapes=[
+            V((4, channels, share), bf16), V((4, channels, share), f32), V((micros, pixels, channels), bf16),
+            V((micros, pixels, channels), f32), V((512, TAPS * share), f32), V((64, 128), f32),
+            pltpu.SemaphoreType.DMA((40,)),
+        ],
+        compiler_params=pltpu.CompilerParams(vmem_limit_bytes=60 * 2**20),
+    )(*parts)
     return (
         logits.reshape(micros, tile_rows, tile_cols, classes),
         feature_grad.reshape(features.shape),
-        branch_grad.astype(f32),
-        small[56:60],
-        small[60:64],
+        branch_grad,
+        gains,
+        biases,
         conv_grad,
-        small[49],
-        small[48],
-        small[:classes].T,
-        small[24:24 + classes, 0],
+        gain.reshape(-1),
+        bias.reshape(-1),
+        weight.T,
+        class_grad.reshape(-1),
     )
 
 

time: 190 us -> 152 us (0.80); the launches traced: 186 us -> 152 us
  Pallas kernels: 167 us -> 151 us
  local copies, waits for them, and re-layouts: 13.3 us -> 0 us
  other arithmetic: 5.65 us -> 0 us
    pallas_call x1 -> x2, Pallas kernels: 167 us -> 151 us  [the longest x1 144 us: canvas_body(): pl.pallas_call(head_kernel, out_shape=(jax.ShapeDtypeStruct((micros, pixe...]
    convert_element_type x2 -> x0, other arithmetic: 4.03 us -> none  [the longest x1 4.02 us: canvas_body(): branch_grad.astype(f32)]
    slice x7 -> x0, local copies, waits for them, and re-layouts: 3.98 us -> none  [the longest x1 1.34 us: canvas_body(): small[60:64]]
    unnamed x9 -> x0, local copies, waits for them, and re-layouts: 3.17 us -> none
where the time goes in v2:
time: 152 us
  Pallas kernels  151 us (99%)
    pallas_call x1, Pallas kernels, canvas_body(): pl.pallas_call(head_kernel, out_shape=(jax.ShapeDtypeStruct((micros, pixe...  144 us
    pallas_call x1, Pallas kernels, canvas_body(): pl.pallas_call(place_kernel, out_shape=(jax.ShapeDtypeStruct((micros, pix...  6.94 us

profile of v2, /device:TPU:8, one launch (start us, length us, event | category | flops | bytes accessed | tf_op | source)
XLA Modules:
  0.0 151.5 jit_solution(13906311871851980300)
XLA Ops:
  0.6 143.7 %shard_map.204 = (f32[2,64,19]{2,1,0:T(8,128)}, bf16[2,64,2048]{2,1,0:T(8,128)(2,1)}, bf16[4,2048,128]{2,1,0:T(8,128)(2,1)}, f32[64,128]{1,0:T(8,128)}, f32[512,1152]{1,0:T(8,128)}) custom-call(s32[3,4,8]{2,1,0:T(4,128)} %bitcast.16, f32[4,8,128]{2,1,0:T(8,128)} %constant.4.clone.lane_table, f32[176,8]{1,0:T(8,128)} %constant.5.clone.row_table, ...), custom_call_target="tpu_custom_call" | custom-call | tf_op jit(solution)/shard_map/pallas_call | solution.py:1245
  144.4 6.9 %shard_map.205 = (f32[2,64,19]{2,1,0:T(8,128)}, f32[2,64,2048]{2,1,0:T(8,128)}, f32[4,2048,128]{2,1,0:T(8,128)}, f32[4,128]{1,0:T(4,128)}, f32[4,128]{1,0:T(4,12...) custom-call(f32[2,64,19]{2,1,0:T(8,128)} %get-tuple-element.25.logit, ...), custom_call_target="tpu_custom_call" | custom-call | tf_op jit(solution)/shard_map/pallas_call | solution.py:1265

commit v3 on v2

--- a/solution.py
+++ b/solution.py
@@ -398,17 +398,10 @@
 
         pl.when((z < 3) if up else (z > 0))(start)
 
-    pool(z)
-    h_send, h_recv = names.take(3), names.take(3)
-    po_copies = [copy(po.at[z], po.at[z], h_send + j - 1, h_recv + j - 1, zpeer(j)) for j in (1, 2, 3)]
-
     @pl.when(w == 0)
     def _():
-        each(po_copies, "start")()
         pass_on(0, 0)
         pass_on(0, 1)
-
-    finals.append(lambda: pl.when(w == 0)(each(po_copies, "wait_send")))
 
     arrive("seed")
     sd[z] = seeds[w] + seed_in[0]
@@ -424,6 +417,7 @@
 
     due["sd"] = sd_wait
 
+    pool(z)
     branch_products(z)
     conv_add(z, x[z], 0)
 
@@ -505,10 +499,7 @@
         for kx, ky in chips:
             conv_copy(c, kx, ky).start()
 
-    def far(c):
-        return (c + z == 3) & ((c == 0) | (c == 3))
-
-    def levels(core):
+    def levels():
         each(bo_copies, "wait_recv")()
         for part in range(4):
             for half in range(2):
@@ -517,23 +508,10 @@
         def level_conv(c, carry):
             lv[c] = dot(u2[c], bo2[c]).astype(bf16)
             conv_add(c, lv[c], 1)
-            if core == 0:
-                pl.when(jnp.logical_not(far(c)))(lambda: conv_send(c))
-            else:
-                conv_send(c)
+            conv_send(c)
             return carry
 
         lax.fori_loop(0, 4, level_conv, 0)
-
-    @pl.when(w == 0)
-    def _():
-        def one(j, carry):
-            src = lax.rem(z + 4 - j, 4)
-            copy(po.at[src], po.at[src], h_send + j - 1, h_recv + j - 1, zpeer(j)).wait_recv()
-            branch_products(src)
-            return carry
-
-        lax.fori_loop(1, 4, one, 0)
 
     @pl.when((w == 1) & (zm == 0))
     def _():
@@ -546,12 +524,8 @@
         own_turn(True)
 
     def arrived(c):
-        @pl.when(w == 1)
-        def _():
-            pool(c)
-            branch_products(c)
-
-        pl.when(w == 0)(lambda: conv_add(c, x[c], 0))
+        pool(c)
+        branch_products(c)
 
     for k in (1, 2, 3):
         if k < 3:
@@ -562,24 +536,16 @@
                 pass_on(k, h)
         pl.when(z >= k)(lambda: arrived(z - k))
         pl.when(z + k <= 3)(lambda: arrived(z + k))
-        if k == 1:
-            pl.when(w == 0)(branch_norm)
-        if k == 2:
-            pl.when(w == 0)(lambda: levels(0))
-
-    pl.when((w == 0) & far(3 - z))(lambda: conv_send(3 - z))
-
-    @pl.when(w == 1)
-    def _():
-        branch_norm()
-
-        def late(j, carry):
-            c = lax.rem(z + j, 4)
-            conv_add(c, x[c], 0)
-            return carry
-
-        lax.fori_loop(1, 4, late, 0)
-        levels(1)
+
+    branch_norm()
+
+    def late(j, carry):
+        c = lax.rem(z + j, 4)
+        conv_add(c, x[c], 0)
+        return carry
+
+    lax.fori_loop(1, 4, late, 0)
+    levels()
 
     conv_copies = [conv_copy(c, kx, ky) for c in range(4) for kx, ky in chips]
     due["conv"] = each(conv_copies, "wait_recv")
@@ -887,6 +853,21 @@
 
     lax.fori_loop(0, 4, split_rows, 0)
 
+    def pooled_grad(c, carry):
+        for level in range(4):
+            rows = slice(STARTS[level], STARTS[level] + SPANS[level])
+            gps[c, rows, :] = dot(gpx[c, rows, :], wb2[level], BOTH_LAST).astype(bf16)
+        return carry
+
+    lax.fori_loop(0, 4, pooled_grad, 0)
+    p_send, p_recv = names.take(3), names.take(3)
+    gp_copies = [
+        copy(gps.at[lax.rem(z + j, 4)], gpr.at[j - 1], p_send + j - 1, p_recv + j - 1, zpeer(j)) for j in (1, 2, 3)
+    ]
+    each(gp_copies, "start")()
+    due["gp"] = each(gp_copies, "wait_recv")
+    finals.append(each(gp_copies, "wait_send"))
+
     for level in range(4):
         rows = slice(STARTS[level], STARTS[level] + SPANS[level])
         total = None
@@ -901,21 +882,6 @@
     bg_copy.start()
     due["bgc"] = bg_copy.wait_recv
     finals.append(bg_copy.wait_send)
-
-    def pooled_grad(c, carry):
-        for level in range(4):
-            rows = slice(STARTS[level], STARTS[level] + SPANS[level])
-            gps[c, rows, :] = dot(gpx[c, rows, :], wb2[level], BOTH_LAST).astype(bf16)
-        return carry
-
-    lax.fori_loop(0, 4, pooled_grad, 0)
-    p_send, p_recv = names.take(3), names.take(3)
-    gp_copies = [
-        copy(gps.at[lax.rem(z + j, 4)], gpr.at[j - 1], p_send + j - 1, p_recv + j - 1, zpeer(j)) for j in (1, 2, 3)
-    ]
-    each(gp_copies, "start")()
-    due["gp"] = each(gp_copies, "wait_recv")
-    finals.append(each(gp_copies, "wait_send"))
 
     bg_wait = due.pop("bgc")
     own_channels = pl.ds(pl.multiple_of(512 * g + 256 * w, 256), 256)

time: 152 us -> 151 us (level)
  no operation moved by 1% of the time
where the time goes in v3:
time: 151 us
  Pallas kernels  150 us (99%)
    pallas_call x1, Pallas kernels, canvas_body(): pl.pallas_call(head_kernel, out_shape=(jax.ShapeDtypeStruct((micros, pixe...  143 us
    pallas_call x1, Pallas kernels, canvas_body(): pl.pallas_call(place_kernel, out_shape=(jax.ShapeDtypeStruct((micros, pix...  6.94 us

profile of v3, /device:TPU:8, one launch (start us, length us, event | category | flops | bytes accessed | tf_op | source)
XLA Modules:
  0.0 150.8 jit_solution(1361865308099024513)
XLA Ops:
  0.6 143.0 %shard_map.204 = (f32[2,64,19]{2,1,0:T(8,128)}, bf16[2,64,2048]{2,1,0:T(8,128)(2,1)}, bf16[4,2048,128]{2,1,0:T(8,128)(2,1)}, f32[64,128]{1,0:T(8,128)}, f32[512,1152]{1,0:T(8,128)}) custom-call(s32[3,4,8]{2,1,0:T(4,128)} %bitcast.16, f32[4,8,128]{2,1,0:T(8,128)} %constant.4.clone.lane_table, f32[176,8]{1,0:T(8,128)} %constant.5.clone.row_table, ...), custom_call_target="tpu_custom_call" | custom-call | tf_op jit(solution)/shard_map/pallas_call | solution.py:1211
  143.6 6.9 %shard_map.205 = (f32[2,64,19]{2,1,0:T(8,128)}, f32[2,64,2048]{2,1,0:T(8,128)}, f32[4,2048,128]{2,1,0:T(8,128)}, f32[4,128]{1,0:T(4,128)}, f32[4,128]{1,0:T(4,12...) custom-call(f32[2,64,19]{2,1,0:T(8,128)} %get-tuple-element.25.logit, ...), custom_call_target="tpu_custom_call" | custom-call | tf_op jit(solution)/shard_map/pallas_call | solution.py:1231

commit v4 on v3

--- a/solution.py
+++ b/solution.py
@@ -843,6 +843,37 @@
     due["lt"] = each(lt_copies, "wait_recv")
     finals.append(each(lt_copies, "wait_send"))
 
+    weight_grad(yq, 1 - w)
+    pl.when(w == 1)(lambda: dw_copy.start())
+
+    def dw_sum():
+        @pl.when(w == 0)
+        def _():
+            dw_copy.wait_recv()
+            dw[1] = dw[1] + dwr[...]
+            pl.when(yq == 0)(lambda: cg_out(dw.at[1]).start())
+            pl.when(yq == 1)(lambda: dw_back.start())
+
+    def dw_place():
+        @pl.when((w == 1) & (yq == 1))
+        def _():
+            dw_back.wait_recv()
+            cg_out(dwr).start()
+
+        dw_copy.wait_send()
+
+        @pl.when(w != yq)
+        def _():
+            dw_y.wait_recv()
+            dw[0] = dwx[...].astype(f32)
+            cg_out(dw.at[0]).start()
+
+    due["dw"] = dw_sum
+    due["dwy"] = dw_place
+    finals.append(lambda: cg_out(dw.at[0]).wait())
+    finals.append(lambda: pl.when(w == 1)(lambda: dw_y.wait_send()))
+    finals.append(lambda: pl.when((w == 0) & (yq == 1))(lambda: dw_back.wait_send()))
+
     arrive("gpre")
 
     def split_rows(c, carry):
@@ -917,37 +948,6 @@
     middle_send(2)
     finals.append(scatter_sent)
 
-    weight_grad(yq, 1 - w)
-    pl.when(w == 1)(lambda: dw_copy.start())
-
-    def dw_sum():
-        @pl.when(w == 0)
-        def _():
-            dw_copy.wait_recv()
-            dw[1] = dw[1] + dwr[...]
-            pl.when(yq == 0)(lambda: cg_out(dw.at[1]).start())
-            pl.when(yq == 1)(lambda: dw_back.start())
-
-    def dw_place():
-        @pl.when((w == 1) & (yq == 1))
-        def _():
-            dw_back.wait_recv()
-            cg_out(dwr).start()
-
-        dw_copy.wait_send()
-
-        @pl.when(w != yq)
-        def _():
-            dw_y.wait_recv()
-            dw[0] = dwx[...].astype(f32)
-            cg_out(dw.at[0]).start()
-
-    due["dw"] = dw_sum
-    due["dwy"] = dw_place
-    finals.append(lambda: cg_out(dw.at[0]).wait())
-    finals.append(lambda: pl.when(w == 1)(lambda: dw_y.wait_send()))
-    finals.append(lambda: pl.when((w == 0) & (yq == 1))(lambda: dw_back.wait_send()))
-
     s_send, s_recv = names.take(7), names.take(7)
 
     def small_copy(n):
@@ -1085,7 +1085,7 @@
 def place_kernel(
     logits, fgrad, bgrad, small, cgrad,
     logits_out, fgrad_out, bgrad_out, gains_out, biases_out, cgrad_out, gain_out, bias_out, weight_out, class_out,
-    low, wide, feats, feats_wide, taps, square, sems,
+    low, wide, feats, feats_wide, taps, by_tap, square, sems,
 ):
     levels, classes, micros = bgrad.shape[0], class_out.shape[1], fgrad.shape[0]
     half = bgrad.shape[1] // 2
@@ -1103,7 +1103,7 @@
         pltpu.make_async_copy(feats_wide.at[m], fgrad_out.at[m], sems.at[first + count + m]) for m in range(micros)
     ]
     tap_stores = [
-        pltpu.make_async_copy(taps.at[:, pl.ds(128 * t, 128)], cgrad_out.at[t], sems.at[first + count + micros + t])
+        pltpu.make_async_copy(by_tap.at[t], cgrad_out.at[t], sems.at[first + count + micros + t])
         for t in range(TAPS)
     ]
     for n, p in enumerate(pieces):
@@ -1115,7 +1115,8 @@
         feats_wide[m] = feats[m].astype(jnp.float32)
         stores[count + m].start()
     tap_load.wait()
-    for store in tap_stores:
+    for t, store in enumerate(tap_stores):
+        by_tap[t] = taps[:, 128 * t:128 * t + 128]
         store.start()
     logits_out[...] = logits[...]
     gains_out[...] = small[56:60, :]
@@ -1246,7 +1247,7 @@
         out_specs=(vmem, hbm, hbm, vmem, vmem, hbm, vmem, vmem, vmem, vmem),
         scratch_shapes=[
             V((4, channels, share), bf16), V((4, channels, share), f32), V((micros, pixels, channels), bf16),
-            V((micros, pixels, channels), f32), V((512, TAPS * share), f32), V((64, 128), f32),
+            V((micros, pixels, channels), f32), V((512, TAPS * share), f32), V((TAPS, 512, share), f32), V((64, 128), f32),
             pltpu.SemaphoreType.DMA((40,)),
         ],
         compiler_params=pltpu.CompilerParams(vmem_limit_bytes=60 * 2**20),

time: 151 us -> 151 us (level)
  no operation moved by 1% of the time
where the time goes in v4:
time: 151 us
  Pallas kernels  150 us (99%)
    pallas_call x1, Pallas kernels, canvas_body(): pl.pallas_call(head_kernel, out_shape=(jax.ShapeDtypeStruct((micros, pixe...  143 us
    pallas_call x1, Pallas kernels, canvas_body(): pl.pallas_call(place_kernel, out_shape=(jax.ShapeDtypeStruct((micros, pix...  6.96 us

profile of v4, /device:TPU:8, one launch (start us, length us, event | category | flops | bytes accessed | tf_op | source)
XLA Modules:
  0.0 150.8 jit_solution(4218463500668508254)
XLA Ops:
  0.6 143.0 %shard_map.204 = (f32[2,64,19]{2,1,0:T(8,128)}, bf16[2,64,2048]{2,1,0:T(8,128)(2,1)}, bf16[4,2048,128]{2,1,0:T(8,128)(2,1)}, f32[64,128]{1,0:T(8,128)}, f32[512,1152]{1,0:T(8,128)}) custom-call(s32[3,4,8]{2,1,0:T(4,128)} %bitcast.16, f32[4,8,128]{2,1,0:T(8,128)} %constant.4.clone.lane_table, f32[176,8]{1,0:T(8,128)} %constant.5.clone.row_table, ...), custom_call_target="tpu_custom_call" | custom-call | tf_op jit(solution)/shard_map/pallas_call | solution.py:1212
  143.6 7.0 %shard_map.205 = (f32[2,64,19]{2,1,0:T(8,128)}, f32[2,64,2048]{2,1,0:T(8,128)}, f32[4,2048,128]{2,1,0:T(8,128)}, f32[4,128]{1,0:T(4,128)}, f32[4,128]{1,0:T(4,12...) custom-call(f32[2,64,19]{2,1,0:T(8,128)} %get-tuple-element.25.logit, ...), custom_call_target="tpu_custom_call" | custom-call | tf_op jit(solution)/shard_map/pallas_call | solution.py:1232
